TPU v7x, 32 devices: a whole 2x2x4 slice. The times are simulated.
32 devices in a mesh: dp: 8 (over z, x), ctx: 4 (over y, core).
Axes of the slice: x: 2, y: 2, z: 4, core: 2. Of those that a mesh axis runs over, the one named last changes fastest.
Arguments:
- tokens: bfloat16 [16, 256, 1024], P('dp', 'ctx'), may hold values from -6 to 6
- segments: int32 [16, 256], P('dp', 'ctx'), may hold values from 0 to 15, as said below
- norm_gain: bfloat16 [1024], P(('dp', 'ctx')), may hold values from 0.099609375 to 1.8984375
- in_weight: bfloat16 [1024, 3072], P(('dp', 'ctx')), may hold values from -0.1875 to 0.1875
- conv_taps: bfloat16 [3, 1024], P(None, ('dp', 'ctx')), may hold values from -3 to 3
- out_weight: bfloat16 [1024, 1024], P(('dp', 'ctx')), may hold values from -0.1875 to 0.1875
- ffn_gain: bfloat16 [1024], P(('dp', 'ctx')), may hold values from 0.099609375 to 1.8984375
- gate_weight: bfloat16 [1024, 4608], P(('dp', 'ctx')), may hold values from -0.1875 to 0.1875
- up_weight: bfloat16 [1024, 4608], P(('dp', 'ctx')), may hold values from -0.1875 to 0.1875
- down_weight: bfloat16 [4608, 1024], P(('dp', 'ctx')), may hold values from -0.09375 to 0.09375
- cotangent: bfloat16 [16, 256, 1024], P('dp', 'ctx'), may hold values from -6 to 6
Outputs:
- mixed: bfloat16 [16, 256, 1024], P('dp', 'ctx')
- input_grad: float32 [16, 256, 1024], P('dp', 'ctx')
- grad_norm_gain: float32 [1024], P(('dp', 'ctx'))
- grad_in_weight: float32 [1024, 3072], P(('dp', 'ctx'))
- grad_conv_taps: float32 [3, 1024], P(None, ('dp', 'ctx'))
- grad_out_weight: float32 [1024, 1024], P(('dp', 'ctx'))
- grad_ffn_gain: float32 [1024], P(('dp', 'ctx'))
- grad_gate_weight: float32 [1024, 4608], P(('dp', 'ctx'))
- grad_up_weight: float32 [1024, 4608], P(('dp', 'ctx'))
- grad_down_weight: float32 [4608, 1024], P(('dp', 'ctx'))
Inputs may be any that keep to these rules, and one draw needn't show every extreme that they name: `segments`: within each sequence the numbers start at 0 at its first position and rise by one at the first position of each new document. Among the 2 sequences of one index of dp, one drawn from the seed holds a single document; every other sequence holds exactly 16 documents.
All inputs are finite; a program needn't handle non-finite values.
Results may differ from a plain program's by a relative error of at most 0.0092.
Values may be sent and summed in bfloat16 or wider, within the bound.
No kernel may reach another device: no remote copies, remote signals or barrier semaphores. Data moves between devices by JAX's collectives and lax.ppermute only.
A program may use at most 320 MiB of HBM per device.

v0:
```python
import math

import jax
import jax.numpy as jnp
from jax import lax
from jax.sharding import PartitionSpec as P

EPS = 1e-05


def passed_along(value, axis, steps):
    count = lax.axis_size(axis)
    initial, last = (max(0, -steps), min(count, count - steps))
    return lax.ppermute(value, axis, [(source, source + steps) for source in range(initial, last)])


def cut_along(value, dim, devices):
    before, after = (value.shape[:dim], value.shape[dim + 1 :])
    return jnp.moveaxis(value.reshape(*before, devices, -1, *after), dim, 0)


def sum_at_owner(value, axis, dim):
    tiles = cut_along(value, dim, lax.axis_size(axis))
    arrived = lax.all_to_all(tiles, axis, split_axis=0, concat_axis=0, tiled=True)
    return arrived.astype(jnp.float32).sum(axis=0)


def sent_together(arrays, axis, dim, along):
    widths = [math.prod(a.shape[along:]) for a in arrays]
    both = jnp.concatenate(
        [a.reshape(*a.shape[:along], w) for a, w in zip(arrays, widths)], axis=along
    )
    result = sum_at_owner(both, axis, dim)
    tiles = jnp.split(result, [sum(widths[:k]) for k in range(1, len(widths))], axis=along)
    return tuple(
        (b.reshape(*result.shape[:along], *a.shape[along:]) for a, b in zip(arrays, tiles))
    )


def scale_rows(values):
    return lax.rsqrt(jnp.mean(values * values, axis=-1, keepdims=True) + EPS)


def across(left_operand, right_operand):
    return lax.dot_general(
        left_operand, right_operand, (((0,), (0,)), ((), ())), preferred_element_type=jnp.float32
    )


def against(left_operand, right_operand):
    return lax.dot_general(
        left_operand, right_operand, (((1,), (1,)), ((), ())), preferred_element_type=jnp.float32
    )


def norm_back(grad_normed, normed, inverse):
    return inverse * (grad_normed - normed * jnp.mean(grad_normed * normed, axis=-1, keepdims=True))


def by_owner(values, dp_count, ctx_count):
    width = values.shape[-1]
    return values.reshape(
        values.shape[:-1] + (dp_count, ctx_count, width // (dp_count * ctx_count))
    )


def owner_rows(values):
    return values.reshape(values.shape[0], values.shape[1] * values.shape[3])


def on_device(
    tokens,
    segments,
    norm_gain,
    in_weight,
    conv_taps,
    out_weight,
    ffn_gain,
    gate_weight,
    up_weight,
    down_weight,
    cotangent,
):
    seq_count, seq_rows, features = tokens.shape
    all_rows = seq_count * seq_rows
    dp_count = lax.axis_size("dp")
    ctx_count = lax.axis_size("ctx")
    full_gain1, full_in, full_taps, full_out, full_gain2, complete_gate, full_up, full_down = (
        lax.all_gather(norm_gain, ("dp", "ctx"), axis=0, tiled=True),
        lax.all_gather(in_weight, ("dp", "ctx"), axis=0, tiled=True),
        lax.all_gather(conv_taps, ("dp", "ctx"), axis=1, tiled=True),
        lax.all_gather(out_weight, ("dp", "ctx"), axis=0, tiled=True),
        lax.all_gather(ffn_gain, ("dp", "ctx"), axis=0, tiled=True),
        lax.all_gather(gate_weight, ("dp", "ctx"), axis=0, tiled=True),
        lax.all_gather(up_weight, ("dp", "ctx"), axis=0, tiled=True),
        lax.all_gather(down_weight, ("dp", "ctx"), axis=0, tiled=True),
    )
    token_rows = tokens.reshape(all_rows, features).astype(jnp.float32)
    inverse1 = scale_rows(token_rows)
    normed1 = token_rows * inverse1
    gain_one = full_gain1.astype(jnp.float32)
    hidden_in = (normed1 * gain_one).astype(jnp.bfloat16)
    projected = jnp.dot(hidden_in, full_in, preferred_element_type=jnp.float32)
    part_b = projected[:, :features]
    part_c = projected[:, features : 2 * features]
    part_x = projected[:, 2 * features :]
    mixed_in = (part_b * part_x).astype(jnp.bfloat16).reshape(seq_count, seq_rows, features)
    seg_rim = passed_along(segments[:, seq_rows - 2 :], "ctx", 1)
    mix_rim = passed_along(mixed_in[:, seq_rows - 2 :, :], "ctx", 1)
    seg_ext = jnp.concatenate([seg_rim, segments], axis=1)
    keep_one = (seg_ext[:, 1 : seq_rows + 1] == segments).astype(jnp.float32)[:, :, None]
    keep_two = (seg_ext[:, :seq_rows] == segments).astype(jnp.float32)[:, :, None]
    mix_ext = jnp.concatenate([mix_rim, mixed_in], axis=1).astype(jnp.float32)
    current = mix_ext[:, 2:]
    previous = mix_ext[:, 1 : seq_rows + 1]
    earlier = mix_ext[:, :seq_rows]
    tap_values = full_taps.astype(jnp.float32)
    shortconv = (
        tap_values[2] * current
        + tap_values[1] * previous * keep_one
        + tap_values[0] * earlier * keep_two
    )
    short_flat = shortconv.reshape(all_rows, features)
    gated = (part_c * short_flat).astype(jnp.bfloat16)
    branch_path = jnp.dot(gated, full_out, preferred_element_type=jnp.float32)
    resid = token_rows + branch_path
    inverse2 = scale_rows(resid)
    normed2 = resid * inverse2
    gain_two = full_gain2.astype(jnp.float32)
    hidden_ffn = (normed2 * gain_two).astype(jnp.bfloat16)
    gate_act = jnp.dot(hidden_ffn, complete_gate, preferred_element_type=jnp.float32)
    upward = jnp.dot(hidden_ffn, full_up, preferred_element_type=jnp.float32)
    sigmoid_gate = jax.nn.sigmoid(gate_act)
    swish_gate = gate_act * sigmoid_gate
    hidden = (swish_gate * upward).astype(jnp.bfloat16)
    mixed = (resid + jnp.dot(hidden, full_down, preferred_element_type=jnp.float32)).astype(
        jnp.bfloat16
    )
    col_hin, col_gated, column_hidden_feedforward, col_hidden = (
        lax.all_to_all(
            by_owner(hidden_in, dp_count, ctx_count), "ctx", split_axis=2, concat_axis=0, tiled=True
        ),
        lax.all_to_all(
            by_owner(gated, dp_count, ctx_count), "ctx", split_axis=2, concat_axis=0, tiled=True
        ),
        lax.all_to_all(
            by_owner(hidden_ffn, dp_count, ctx_count),
            "ctx",
            split_axis=2,
            concat_axis=0,
            tiled=True,
        ),
        lax.all_to_all(
            by_owner(hidden, dp_count, ctx_count), "ctx", split_axis=2, concat_axis=0, tiled=True
        ),
    )
    col_hin = owner_rows(col_hin)
    col_gated = owner_rows(col_gated)
    column_hidden_feedforward = owner_rows(column_hidden_feedforward)
    col_hidden = owner_rows(col_hidden)
    full_gain2, complete_gate, full_up, full_down = (
        lax.all_gather(ffn_gain, ("dp", "ctx"), axis=0, tiled=True),
        lax.all_gather(gate_weight, ("dp", "ctx"), axis=0, tiled=True),
        lax.all_gather(up_weight, ("dp", "ctx"), axis=0, tiled=True),
        lax.all_gather(down_weight, ("dp", "ctx"), axis=0, tiled=True),
    )
    gain_two = full_gain2.astype(jnp.float32)
    seed_rows = cotangent.reshape(all_rows, features)
    grad_hidden = against(seed_rows, full_down)
    grad_gate = (
        grad_hidden * upward * sigmoid_gate * (1.0 + gate_act * (1.0 - sigmoid_gate))
    ).astype(jnp.bfloat16)
    grad_up = (grad_hidden * swish_gate).astype(jnp.bfloat16)
    grad_hffn = against(grad_gate, complete_gate) + against(grad_up, full_up)
    grad_gain2 = jnp.sum(grad_hffn * normed2, axis=0)
    grad_resid = seed_rows.astype(jnp.float32) + norm_back(grad_hffn * gain_two, normed2, inverse2)
    seed_all, gate_all, up_all = (
        lax.all_gather(seed_rows, "ctx", axis=0, tiled=True),
        lax.all_gather(grad_gate, "ctx", axis=0, tiled=True),
        lax.all_gather(grad_up, "ctx", axis=0, tiled=True),
    )
    shard_down_weight = across(col_hidden, seed_all)
    local_gate = across(column_hidden_feedforward, gate_all)
    local_up = across(column_hidden_feedforward, up_all)
    owned_gate, owned_up, owned_down = (
        lax.psum_scatter(local_gate, "dp", scatter_dimension=0, tiled=True),
        lax.psum_scatter(local_up, "dp", scatter_dimension=0, tiled=True),
        lax.psum_scatter(shard_down_weight, "dp", scatter_dimension=0, tiled=True),
    )
    full_gain1, full_in, full_taps, full_out = (
        lax.all_gather(norm_gain, ("dp", "ctx"), axis=0, tiled=True),
        lax.all_gather(in_weight, ("dp", "ctx"), axis=0, tiled=True),
        lax.all_gather(conv_taps, ("dp", "ctx"), axis=1, tiled=True),
        lax.all_gather(out_weight, ("dp", "ctx"), axis=0, tiled=True),
    )
    gain_one = full_gain1.astype(jnp.float32)
    tap_values = full_taps.astype(jnp.float32)
    grad_branch = grad_resid.astype(jnp.bfloat16)
    grad_gated = against(grad_branch, full_out)
    grad_short = (
        (grad_gated * part_c)
        .astype(jnp.bfloat16)
        .reshape(seq_count, seq_rows, features)
        .astype(jnp.float32)
    )
    grad_taps = jnp.stack(
        [
            jnp.sum(grad_short * earlier * keep_two, axis=(0, 1)),
            jnp.sum(grad_short * previous * keep_one, axis=(0, 1)),
            jnp.sum(grad_short * current, axis=(0, 1)),
        ]
    )
    weighted_one = grad_short * keep_one
    weighted_two = grad_short * keep_two
    rim_send = jnp.stack(
        [
            tap_values[0] * weighted_two[:, 0],
            tap_values[1] * weighted_one[:, 0] + tap_values[0] * weighted_two[:, 1],
        ],
        axis=1,
    )
    rim_back = passed_along(rim_send, "ctx", -1)
    blank_one = jnp.zeros((seq_count, 1, features), jnp.float32)
    empty_second = jnp.zeros((seq_count, 2, features), jnp.float32)
    blank_rest = jnp.zeros((seq_count, seq_rows - 2, features), jnp.float32)
    grad_mixed = (
        tap_values[2] * grad_short
        + tap_values[1] * jnp.concatenate([weighted_one[:, 1:], blank_one], axis=1)
        + tap_values[0] * jnp.concatenate([weighted_two[:, 2:], empty_second], axis=1)
    )
    grad_mixed = grad_mixed + jnp.concatenate([blank_rest, rim_back], axis=1)
    grad_mixed = grad_mixed.reshape(all_rows, features)
    grad_proj = jnp.concatenate(
        [grad_mixed * part_x, grad_gated * short_flat, grad_mixed * part_b], axis=1
    ).astype(jnp.bfloat16)
    grad_hin = against(grad_proj, full_in)
    grad_gain1 = jnp.sum(grad_hin * normed1, axis=0)
    input_grad = grad_resid + norm_back(grad_hin * gain_one, normed1, inverse1)
    branch_all, proj_all = (
        lax.all_gather(grad_branch, "ctx", axis=0, tiled=True),
        lax.all_gather(grad_proj, "ctx", axis=0, tiled=True),
    )
    local_out = across(col_gated, branch_all)
    local_in = across(col_hin, proj_all)
    group_gain1, group_gain2, group_taps = (
        lax.psum_scatter(
            by_owner(grad_gain1, dp_count, ctx_count), "ctx", scatter_dimension=1, tiled=True
        ),
        lax.psum_scatter(
            by_owner(grad_gain2, dp_count, ctx_count), "ctx", scatter_dimension=1, tiled=True
        ),
        lax.psum_scatter(
            by_owner(grad_taps, dp_count, ctx_count), "ctx", scatter_dimension=2, tiled=True
        ),
    )
    group_gain1 = group_gain1.reshape(-1)
    group_gain2 = group_gain2.reshape(-1)
    group_taps = group_taps.reshape(group_taps.shape[0], -1)
    owned_gain1, owned_in, owned_taps, owned_out, owned_gain2 = (
        *sent_together(
            (group_gain1.astype(jnp.bfloat16), local_in.astype(jnp.bfloat16)), "dp", 0, 1
        ),
        sum_at_owner(group_taps.astype(jnp.bfloat16), "dp", 1),
        *sent_together(
            (local_out.astype(jnp.bfloat16), group_gain2.astype(jnp.bfloat16)), "dp", 0, 1
        ),
    )
    return (
        mixed.reshape(seq_count, seq_rows, features),
        input_grad.reshape(seq_count, seq_rows, features),
        owned_gain1,
        owned_in,
        owned_taps,
        owned_out,
        owned_gain2,
        owned_gate,
        owned_up,
        owned_down,
    )


def solution(mesh):
    in_specs = (
        P("dp", "ctx", None),
        P("dp", "ctx"),
        P(("dp", "ctx")),
        P(("dp", "ctx"), None),
        P(None, ("dp", "ctx")),
        P(("dp", "ctx"), None),
        P(("dp", "ctx")),
        P(("dp", "ctx"), None),
        P(("dp", "ctx"), None),
        P(("dp", "ctx"), None),
        P("dp", "ctx", None),
    )
    out_specs = (
        P("dp", "ctx", None),
        P("dp", "ctx", None),
        P(("dp", "ctx")),
        P(("dp", "ctx"), None),
        P(None, ("dp", "ctx")),
        P(("dp", "ctx"), None),
        P(("dp", "ctx")),
        P(("dp", "ctx"), None),
        P(("dp", "ctx"), None),
        P(("dp", "ctx"), None),
    )
    return jax.shard_map(
        on_device, mesh=mesh, in_specs=in_specs, out_specs=out_specs, check_vma=False
    )
```

profile of v0, /device:TPU:0, one launch (start us, length us, event | category | flops | bytes accessed | tf_op | source)
XLA Modules:
  0.0 913.4 jit_solution(11790032886545448123)
XLA Ops:
  11.4 2.3 collective-permute-start.1
  14.9 1.8 convert_element_type.165
  17.2 41.9 %all-reduce.9 = (bf16[1024]{0:T(1024)(128)(2,1)S(1)}, bf16[1024]{0:T(1024)(128)(2,1)S(1)}) all-reduce(bf16[1024]{0:T(1024)(128)(2,1)S(1)} %dynamic-update-slice, bf16[1024]{0:T(1024)(128)(2,1)S(1)} %dynamic-update-slice.1), channel_id=1, replica_groups=mesh['dp'=8,'ctx'=4] {'dp','ctx'}, use_global_device_ids=true, to_apply=%add.3 | all-reduce | flops 2048 | bytes 8192
  59.1 40.9 %all-gather = bf16[32,32,3]{1,2,0:T(4,128)(2,1)S(1)} all-gather(bf16[1,32,3]{1,2,0:T(4,128)(2,1)S(1)} %bitcast.162), channel_id=1, replica_groups=mesh['dp'=8,'ctx'=4] {'dp','ctx'}, dimensions={0}, use_global_device_ids=true | all-gather | bytes 6336 | tf_op jit(solution)/shard_map/all_gather | solution.py:91
  100.4 3.8 fusion.33
  104.2 2.2 collective-permute-start
  107.7 33.6 %all-gather.14.cloned.1.call-done = bf16[1024,1024]{1,0:T(8,128)(2,1)} async-done(((bf16[32,1024]{1,0:T(8,128)(2,1)}), bf16[1024,1024]{1,0:T(8,128)(2,1)}) %all-gather.14.cloned.1.call-update) | async-done | bytes 2097168 | tf_op jit(solution)/shard_map/all_gather | solution.py:92
  141.3 2.2 multiply_reduce_fusion.4
  143.6 81.5 %all-gather.16.cloned.1.call-done = bf16[1024,4608]{1,0:T(8,128)(2,1)} async-done(((bf16[32,4608]{1,0:T(8,128)(2,1)}), bf16[1024,4608]{1,0:T(8,128)(2,1)}) %all-gather.16.cloned.1.call-update) | async-done | bytes 9437200 | tf_op jit(solution)/shard_map/all_gather | solution.py:94
  225.2 6.5 fusion.34
  231.7 76.9 %all-gather.18.cloned.1.call-done = bf16[1024,4608]{1,0:T(8,128)(2,1)} async-done(((bf16[32,4608]{1,0:T(8,128)(2,1)}), bf16[1024,4608]{1,0:T(8,128)(2,1)}) %all-gather.18.cloned.1.call-update) | async-done | bytes 9437200 | tf_op jit(solution)/shard_map/all_gather | solution.py:95
  308.6 6.5 fusion.35
  315.1 77.0 %all-gather.20.cloned.1.call-done = bf16[4608,1024]{1,0:T(8,128)(2,1)} async-done(((bf16[144,1024]{1,0:T(8,128)(2,1)}), bf16[4608,1024]{1,0:T(8,128)(2,1)}) %all-gather.20.cloned.1.call-update) | async-done | bytes 9437200 | tf_op jit(solution)/shard_map/all_gather | solution.py:96
  392.0 10.4 %multiply_convert_fusion = (bf16[128,4608]{1,0:T(8,128)(2,1)}, bf16[128,4608]{1,0:T(8,128)(2,1)}, bf16[128,4608]{1,0:T(8,128)(2,1)}) fusion(f32[128,4608]{1,0:T(8,128)} %fusion.34, f32[128,4608]{1,0:T(8,128)} %fusion.35, bf16[128,1024]{1,0:T(8,128)(2,1)S(1)} %bitcast.138, bf16[4608,1024]{1,0:T(8,128)(2,1)} %all-gather.20.cloned.1.call-done), kind=kOutput, calls=%fused_computation.2 | convolution fusion | flops 1216806912 | bytes 17956864 | tf_op jit(solution)/shard_map/dot_general | solution.py:51
  403.5 7.3 fusion.36
  410.8 3.2 multiply_reduce_fusion
  415.8 3.6 fusion.9
  421.2 1.4 collective-permute-start.2
  422.7 1.7 collective-permute-done.2
  429.4 29.6 %all_to_all.75 = bf16[128,8,4,144]{0,3,1,2:T(8,128)(2,1)S(1)} all-to-all(bf16[128,8,4,144]{0,3,1,2:T(8,128)(2,1)S(1)} %copy.79), channel_id=1, replica_groups=mesh['dp'=8,'ctx'=4] {'ctx'}, dimensions={2} | all-to-all | bytes 2359296 | tf_op jit(solution)/shard_map/all_to_all | solution.py:153
  459.1 1.9 copy.80
  461.0 5.2 fusion.2
  466.5 11.2 %all_to_all.76 = bf16[128,8,4,32]{0,3,1,2:T(8,128)(2,1)S(1)} all-to-all(bf16[128,8,4,32]{0,3,1,2:T(8,128)(2,1)S(1)} %copy.76), channel_id=1, replica_groups=mesh['dp'=8,'ctx'=4] {'ctx'}, dimensions={2} | all-to-all | bytes 524288 | tf_op jit(solution)/shard_map/all_to_all | solution.py:146
  477.9 5.9 fusion.19
  483.9 17.5 %all-gather.28.cloned.1.call-done = bf16[512,4608]{1,0:T(8,128)(2,1)} async-done(((bf16[128,4608]{1,0:T(8,128)(2,1)}), bf16[512,4608]{1,0:T(8,128)(2,1)}) %all-gather.28.cloned.1.call-update) | async-done | bytes 4718608 | tf_op jit(solution)/shard_map/all_gather | solution.py:180
  501.4 5.9 fusion.17
  508.5 1.8 reshape.216
  511.3 3.4 all-to-all-start
  515.7 5.1 all-to-all-done
  520.7 3.6 all-to-all-start.3
  525.2 5.0 all-to-all-done.3
  530.5 6.1 multiply_reduce_fusion.1
  536.6 10.5 %all-reduce.8 = (bf16[8,4,32]{2,0,1:T(8,128)(2,1)S(1)}, bf16[8,4,32]{2,0,1:T(8,128)(2,1)S(1)}) all-reduce(f32[8,4,32]{2,0,1:T(8,128)S(1)} %copy.63, f32[8,4,32]{2,0,1:T(8,128)S(1)} %copy.73), channel_id=2, replica_groups=mesh['dp'=8,'ctx'=4] {'ctx'}, use_global_device_ids=true, to_apply=%region_5.0.clone | all-reduce | flops 2048 | bytes 12288
  549.3 5.7 all-to-all-start.2
  555.0 1.7 convolution_convert_fusion.1
  557.6 3.9 all-to-all-done.2
  561.5 3.5 all-to-all-start.4
  565.9 7.1 all-gather.22.cloned.1.call-done
  573.0 2.9 convolution_convert_fusion
  575.9 1.9 pad_maximum_fusion
  577.8 1.7 all-to-all-done.4
  579.4 4.3 all-to-all-start.1
  583.8 6.2 fusion.1
  593.1 65.5 %all-to-all-done.1 = bf16[8,32,3073]{2,1,0:T(8,128)(2,1)} async-done(((bf16[8,32,3073]{2,1,0:T(8,128)(2,1)}), bf16[8,32,3073]{2,1,0:T(8,128)(2,1)}, u32[]{:S(2)}, u32[]{:S(2)}) %all-to-all-start.1) | async-done | bytes 1573408 | tf_op jit(solution)/shard_map/all_to_all | solution.py:24
  658.7 1.7 convert_reduce_fusion
  662.0 45.2 %reduce-scatter.11.cloned.1.call-done = f32[144,1024]{1,0:T(8,128)} async-done(((f32[1152,1024]{1,0:T(8,128)}), f32[144,1024]{1,0:T(8,128)}) %reduce-scatter.11.cloned.1.call-update) | async-done | bytes 589840 | tf_op jit(solution)/shard_map/reduce_scatter | solution.py:188
  707.2 99.9 %reduce-scatter.7.cloned.1.call-done = f32[32,4608]{1,0:T(8,128)} async-done(((f32[256,4608]{1,0:T(8,128)}), f32[32,4608]{1,0:T(8,128)}) %reduce-scatter.7.cloned.1.call-update) | async-done | bytes 589840 | tf_op jit(solution)/shard_map/reduce_scatter | solution.py:186
  807.1 99.8 %reduce-scatter.9.cloned.1.call-done = f32[32,4608]{1,0:T(8,128)} async-done(((f32[256,4608]{1,0:T(8,128)}), f32[32,4608]{1,0:T(8,128)}) %reduce-scatter.9.cloned.1.call-update) | async-done | bytes 589840 | tf_op jit(solution)/shard_map/reduce_scatter | solution.py:187
  (150 shorter events, 30.2 us)
Async XLA Ops:
  7.2 93.1 %copy-start.17 = (s32[2,64]{1,0:T(2,128)S(1)}, s32[2,64]{1,0:T(2,128)}, u32[]{:S(2)}) copy-start(s32[2,64]{1,0:T(2,128)} %param.12) | copy-start | bytes 1540
  7.2 92.9 %copy-start.2 = (bf16[2,64,1024]{2,1,0:T(8,128)(2,1)S(1)}, bf16[2,64,1024]{2,1,0:T(8,128)(2,1)}, u32[]{:S(2)}) copy-start(bf16[2,64,1024]{2,1,0:T(8,128)(2,1)} %param.11) | copy-start | bytes 786436
  7.2 9.5 %copy-start.19 = (bf16[32]{0:T(256)(128)(2,1)S(1)}, bf16[32]{0:T(256)(128)(2,1)}, u32[]{:S(2)}) copy-start(bf16[32]{0:T(256)(128)(2,1)} %param.13) | copy-start | bytes 196
  7.2 9.7 %copy-start.20 = (bf16[32]{0:T(256)(128)(2,1)S(1)}, bf16[32]{0:T(256)(128)(2,1)}, u32[]{:S(2)}) copy-start(bf16[32]{0:T(256)(128)(2,1)} %param.17) | copy-start | bytes 196
  7.2 51.9 %copy-start.18 = (bf16[3,32]{1,0:T(4,128)(2,1)S(1)}, bf16[3,32]{1,0:T(4,128)(2,1)}, u32[]{:S(2)}) copy-start(bf16[3,32]{1,0:T(4,128)(2,1)} %param.15) | copy-start | bytes 580
  7.2 93.1 %all-gather.12.cloned.1.call-start = ((), (), s32[]{:S(2)}) async-start(), calls=%async_computation.11 | async-start | bytes 6488064 | tf_op jit(solution)/shard_map/all_gather | solution.py:90
  8.0 133.3 %all-gather.14.cloned.1.call-start = ((), (), s32[]{:S(2)}) async-start(), calls=%async_computation.12 | async-start | bytes 2162688 | tf_op jit(solution)/shard_map/all_gather | solution.py:92
  8.7 216.4 %all-gather.16.cloned.1.call-start = ((), (), s32[]{:S(2)}) async-start(), calls=%async_computation.13 | async-start | bytes 9732096 | tf_op jit(solution)/shard_map/all_gather | solution.py:94
  9.4 299.1 %all-gather.18.cloned.1.call-start = ((), (), s32[]{:S(2)}) async-start(), calls=%async_computation.14 | async-start | bytes 9732096 | tf_op jit(solution)/shard_map/all_gather | solution.py:95
  10.0 382.0 %all-gather.20.cloned.1.call-start = ((), (), s32[]{:S(2)}) async-start(), calls=%async_computation.15 | async-start | bytes 9732096 | tf_op jit(solution)/shard_map/all_gather | solution.py:96
  10.6 450.4 %all-gather.30.cloned.1.call-start = ((), (), s32[]{:S(2)}) async-start(), calls=%async_computation.22 | async-start | bytes 1310720 | tf_op jit(solution)/shard_map/all_gather | solution.py:178
  11.4 88.9 %collective-permute-start.1 = (s32[2,2]{1,0:T(2,128)S(1)}, s32[2,2]{1,0:T(2,128)S(1)}, u32[]{:S(2)}, u32[]{:S(2)}) collective-permute-start(s32[2,2]{1,0:T(2,128)S(1)} %slice.68), channel_id=1, source_target_pairs={{0,1},{1,2},{2,3},{4,5},{5,6},{6,7},{8,9},{9,10},{10,11},{12,13},{... | collective-permute-start | bytes 56 | tf_op jit(solution)/shard_map/ppermute | solution.py:14
  13.8 464.1 %all-gather.26.cloned.1.call-start = ((), (), s32[]{:S(2)}) async-start(), calls=%async_computation.18 | async-start | bytes 5898240 | tf_op jit(solution)/shard_map/all_gather | solution.py:179
  104.2 3.0 collective-permute-start
  107.6 33.7 %copy-start.3 = (f32[2,64,1024]{2,1,0:T(8,128)}, f32[2,64,1024]{2,1,0:T(8,128)S(1)}, u32[]{:S(2)}) copy-start(f32[2,64,1024]{2,1,0:T(8,128)S(1)} %multiply_add_fusion.2) | copy-start | bytes 1572868
  107.7 35.8 %copy-start.8 = (bf16[128,1024]{1,0:T(8,128)(2,1)}, bf16[128,1024]{1,0:T(8,128)(2,1)S(1)}, u32[]{:S(2)}) copy-start(bf16[128,1024]{1,0:T(8,128)(2,1)S(1)} %fusion.15) | copy-start | bytes 786436
  231.7 160.4 %copy-start.10 = (bf16[2,64,1024]{2,1,0:T(8,128)(2,1)S(1)}, bf16[2,64,1024]{2,1,0:T(8,128)(2,1)}, u32[]{:S(2)}) copy-start(bf16[2,64,1024]{2,1,0:T(8,128)(2,1)} %param.21) | copy-start | bytes 786436
  402.5 98.9 %all-gather.28.cloned.1.call-start = ((), (), s32[]{:S(2)}) async-start(), calls=%async_computation.20 | async-start | bytes 5898240 | tf_op jit(solution)/shard_map/all_gather | solution.py:180
  403.3 144.7 %reduce-scatter.13.cloned.1.call-start = ((), (), s32[]{:S(2)}) async-start(), calls=%async_computation.24 | async-start | bytes 61440
  403.5 7.3 copy-start
  403.5 7.3 copy-start.5
  414.1 0.8 copy-start.6
  420.3 134.7 %all-gather.24.cloned.1.call-start = ((), (), s32[]{:S(2)}) async-start(), calls=%async_computation.17 | async-start | bytes 1310720 | tf_op jit(solution)/shard_map/all_gather | solution.py:240
  420.9 152.1 %all-gather.22.cloned.1.call-start = ((), (), s32[]{:S(2)}) async-start(), calls=%async_computation.16 | async-start | bytes 3932160 | tf_op jit(solution)/shard_map/all_gather | solution.py:241
  420.9 3.6 copy-start.4
  421.0 3.6 copy-start.12
  421.2 3.2 collective-permute-start.2
  424.8 0.7 copy-start.13
  424.8 0.8 copy-start.15
  424.8 1.8 copy-start.1
  426.6 280.6 %reduce-scatter.11.cloned.1.call-start = ((), (), s32[]{:S(2)}) async-start(), calls=%async_computation.23 | async-start | bytes 5308416 | tf_op jit(solution)/shard_map/reduce_scatter | solution.py:188
  466.2 340.9 %reduce-scatter.7.cloned.1.call-start = ((), (), s32[]{:S(2)}) async-start(), calls=%async_computation.19 | async-start | bytes 5308416 | tf_op jit(solution)/shard_map/reduce_scatter | solution.py:186
  483.8 423.0 %reduce-scatter.9.cloned.1.call-start = ((), (), s32[]{:S(2)}) async-start(), calls=%async_computation.21 | async-start | bytes 5308416 | tf_op jit(solution)/shard_map/reduce_scatter | solution.py:187
  507.4 7.4 copy-start.9
  508.5 15.8 %copy-start.21 = (u32[32]{0:T(128)S(1)}, u32[32]{0:T(128)}, u32[]{:S(2)}) copy-start(u32[32]{0:T(128)} %constant.35) | copy-start | bytes 388
  510.4 20.1 %copy-start.14 = (bf16[128,1024]{1,0:T(8,128)(2,1)S(1)}, bf16[128,1024]{1,0:T(8,128)(2,1)}, u32[]{:S(2)}) copy-start(bf16[128,1024]{1,0:T(8,128)(2,1)} %copy-done.13) | copy-start | bytes 786436
  511.3 9.4 %all-to-all-start = ((bf16[128,8,4,32]{0,3,1,2:T(8,128)(2,1)}), bf16[128,8,4,32]{0,3,1,2:T(8,128)(2,1)S(1)}, u32[]{:S(2)}, u32[]{:S(2)}) async-start(bf16[128,8,4,32]{0,3,1,2:T(8,128)(2,1)} %copy.65), calls=%async_computation | async-start | bytes 524288 | tf_op jit(solution)/shard_map/all_to_all | solution.py:140
  520.7 9.4 %all-to-all-start.3 = ((bf16[128,8,4,32]{0,3,1,2:T(8,128)(2,1)}), bf16[128,8,4,32]{0,3,1,2:T(8,128)(2,1)S(1)}, u32[]{:S(2)}, u32[]{:S(2)}) async-start(bf16[128,8,4,32]{0,3,1,2:T(8,128)(2,1)} %copy.71), calls=%async_computation.3 | async-start | bytes 524288 | tf_op jit(solution)/shard_map/all_to_all | solution.py:143
  549.3 12.2 %all-to-all-start.2 = ((bf16[8,3,32]{2,1,0:T(4,128)(2,1)}), bf16[8,3,32]{2,1,0:T(4,128)(2,1)S(1)}, u32[]{:S(2)}, u32[]{:S(2)}) async-start(bf16[8,3,32]{2,1,0:T(4,128)(2,1)} %copy.69), calls=%async_computation.2 | async-start | bytes 16384 | tf_op jit(solution)/shard_map/all_to_all | solution.py:24
  561.5 17.9 %all-to-all-start.4 = ((bf16[8,32,1025]{2,1,0:T(8,128)(2,1)}), bf16[8,32,1025]{2,1,0:T(8,128)(2,1)S(1)}, u32[]{:S(2)}, u32[]{:S(2)}) async-start(bf16[8,32,1025]{2,1,0:T(8,128)(2,1)} %pad_maximum_fusion.2), calls=%async_computation.4 | async-start | bytes 1179648 | tf_op jit(solution)/shard_map/all_to_all | solution.py:24
  579.4 79.2 %all-to-all-start.1 = ((bf16[8,32,3073]{2,1,0:T(8,128)(2,1)}), bf16[8,32,3073]{2,1,0:T(8,128)(2,1)}, u32[]{:S(2)}, u32[]{:S(2)}) async-start(bf16[8,32,3073]{2,1,0:T(8,128)(2,1)} %pad_maximum_fusion), calls=%async_computation.1 | async-start | bytes 3276800 | tf_op jit(solution)/shard_map/all_to_all | solution.py:24
  583.7 6.3 copy-start.7
  583.8 6.3 copy-start.11
  583.8 6.3 copy-start.16
Sparse Core Ops, SparseCore 0:
  11.0 72.5 all-gather.11
  86.4 54.8 all-gather.13
  144.2 80.8 all-gather.15
  227.9 80.6 all-gather.17
  311.4 80.6 all-gather.19
  393.4 15.3 all-gather.29
  410.4 47.4 all-gather.25
  459.4 41.8 all-gather.27
  504.4 19.3 reduce-scatter.12
  525.9 16.8 all-gather.23
  544.4 28.5 all-gather.21
  577.5 129.5 reduce-scatter.10
  711.8 95.2 reduce-scatter.6
  811.6 95.2 reduce-scatter.8
where the time goes:
time: 915 us; the launch traced here: 913 us
  waiting for transfers between devices  627 us (69%)
  blocking collectives  134 us (15%)
  matrix products  77.4 us (8%)
  starting transfers between devices  27.3 us (3%)
  local copies, waits for them, and re-layouts  20 us (2%)
  between operations  14.5 us (2%)
  other arithmetic  13.4 us (1%)
    reduce_scatter x1, waiting for transfers between devices, on_device(): lax.psum_scatter(local_gate, 'dp', scatter_dimension=0, tiled=True)  99.9 us
    reduce_scatter x1, waiting for transfers between devices, on_device(): lax.psum_scatter(local_up, 'dp', scatter_dimension=0, tiled=True)  99.8 us
    all_gather x1, waiting for transfers between devices, on_device(): lax.all_gather(gate_weight, ('dp', 'ctx'), axis=0, tiled=True)  81.5 us
    all_gather x1, waiting for transfers between devices, on_device(): lax.all_gather(down_weight, ('dp', 'ctx'), axis=0, tiled=True)  77 us
    all_gather x1, waiting for transfers between devices, on_device(): lax.all_gather(up_weight, ('dp', 'ctx'), axis=0, tiled=True)  76.9 us
    all_to_all x3, waiting for transfers between devices, sum_at_owner(): lax.all_to_all(tiles, axis, split_axis=0, concat_axis=0, tiled=True)  71.1 us
    unnamed x2, blocking collectives  52.4 us
    reduce_scatter x1, waiting for transfers between devices, on_device(): lax.psum_scatter(shard_down_weight, 'dp', scatter_dimension=0, tiled=True)  45.2 us
  transfers between devices with their start and end apart: 22, of which 16 were waited for; matrix products, arithmetic and copies ran while one was open for 12% of the time, Pallas kernels for 0%

commit v1 on v0

v1 whole, which is shorter than its diff:
```python
import functools

import jax
import jax.numpy as jnp
from jax import lax
from jax.experimental import pallas as pl
from jax.experimental.pallas import tpu as pltpu
from jax.sharding import Mesh
from jax.sharding import PartitionSpec as P

EPS = 1e-05
PLANE = ("near", "ctx")


def mate(value, flip):
    count = lax.axis_size("near") * lax.axis_size("ctx")
    return lax.ppermute(value, PLANE, [(k, k ^ flip) for k in range(count)])


def from_planes(block):
    count = lax.axis_size("far")
    came = [block] + [
        lax.ppermute(block, "far", [(f, (f + s) % count) for f in range(count)])
        for s in range(1, count)
    ]
    came = came[::-1]
    start = lax.rem(2 * count - 1 - lax.axis_index("far"), count) * block.shape[0]
    twice = jnp.concatenate(came + came)
    return lax.dynamic_slice_in_dim(twice, start, count * block.shape[0], axis=0)


def reach(block):
    count = lax.axis_size("near") * lax.axis_size("ctx")
    return [block] + [mate(block, flip) for flip in range(2, count, 2)]


def collect(block):
    same = reach(block)
    return same + [mate(b, 1) for b in same]


def halves(blocks):
    half = len(blocks) // 2
    return jnp.concatenate(blocks[:half]), jnp.concatenate(blocks[half:])


def ffn_rows(steps, count, *refs):
    n2_blocks, seed_blocks = refs[:count], refs[count : 2 * count]
    gate_w, up_w, down_w, n2, seed, hid, dgate, dup, mix, same, other = refs[2 * count :]
    f32, bf = jnp.float32, jnp.bfloat16
    rows = n2_blocks[0].shape[0]
    for k in range(count):

        @pl.when(pl.program_id(0) == k * steps // count)
        def _():
            at = k % (count // steps) * rows
            n2[at : at + rows, :] = n2_blocks[k][...]
            seed[at : at + rows, :] = seed_blocks[k][...]

    x = n2[...]
    gate = jnp.dot(x, gate_w[...], preferred_element_type=f32)
    up = jnp.dot(x, up_w[...], preferred_element_type=f32)
    sig = 1.0 / (1.0 + jnp.exp(-gate))
    swish = gate * sig
    h = (swish * up).astype(bf)
    hid[...] = h
    mix[...] = jnp.dot(h, down_w[...], preferred_element_type=f32).astype(bf)
    d_hidden = against(seed[...], down_w[...])
    dg = (d_hidden * up * sig * (1.0 + gate * (1.0 - sig))).astype(bf)
    du = (d_hidden * swish).astype(bf)
    dgate[...] = dg
    dup[...] = du
    d_n2 = against(dg, gate_w[...]) + against(du, up_w[...])
    half = pl.num_programs(0) // 2

    @pl.when(pl.program_id(0) < half)
    def _():
        same[...] = d_n2

    @pl.when(pl.program_id(0) >= half)
    def _():
        other[...] = d_n2.astype(bf)


def ffn(n2_blocks, seed_blocks, w_gate, w_up, w_down):
    count = len(n2_blocks)
    block, features = n2_blocks[0].shape
    rows = count * block
    part = w_gate.shape[1]
    steps = 4
    tile = rows // steps
    f32, bf = jnp.float32, jnp.bfloat16
    row = lambda width: pl.BlockSpec((tile, width), lambda i: (i, 0))
    whole = lambda w: pl.BlockSpec(w.shape, lambda i: (0, 0))
    operands = (*n2_blocks, *seed_blocks, w_gate, w_up, w_down)
    widths = [features, features, part, part, part, features]
    return pl.pallas_call(
        functools.partial(ffn_rows, steps, count),
        grid=(steps,),
        in_specs=[whole(w) for w in operands],
        out_specs=[row(width) for width in widths]
        + [
            pl.BlockSpec((tile, features), lambda i: (jnp.minimum(i, steps // 2 - 1), 0)),
            pl.BlockSpec((tile, features), lambda i: (jnp.maximum(i - steps // 2, 0), 0)),
        ],
        out_shape=[jax.ShapeDtypeStruct((rows, width), bf) for width in widths]
        + [
            jax.ShapeDtypeStruct((rows // 2, features), f32),
            jax.ShapeDtypeStruct((rows // 2, features), bf),
        ],
        compiler_params=pltpu.CompilerParams(vmem_limit_bytes=48 * 2**20),
        cost_estimate=pl.CostEstimate(
            flops=12 * rows * features * part,
            bytes_accessed=6 * features * part + 14 * rows * features + 6 * rows * part,
            transcendentals=rows * part,
        ),
        name="ffn_rows",
    )(*operands)


def ffn_sums(n2, seed, hid, dgate, dup, g_gate, g_up, g_down, turned):
    @pl.when(pl.program_id(0) == 0)
    def _():
        turned[...] = hid[...].T

    bf = jnp.bfloat16
    g_gate[...] = across(n2[...], dgate[...]).astype(bf)
    g_up[...] = across(n2[...], dup[...]).astype(bf)
    g_down[...] = dot(turned[...], seed[...]).astype(bf)


def weight_sums(n2, seed, hid, dgate, dup):
    rows, features = n2.shape
    part = hid.shape[1]
    tile = features // 4
    bf = jnp.bfloat16
    column = lambda height: pl.BlockSpec((height, tile), lambda i: (0, i))
    whole = pl.BlockSpec((rows, part), lambda i: (0, 0))
    return pl.pallas_call(
        ffn_sums,
        grid=(4,),
        in_specs=[column(rows), column(rows), whole, whole, whole],
        out_specs=[
            pl.BlockSpec((tile, part), lambda i: (i, 0)),
            pl.BlockSpec((tile, part), lambda i: (i, 0)),
            column(part),
        ],
        out_shape=[
            jax.ShapeDtypeStruct((features, part), bf),
            jax.ShapeDtypeStruct((features, part), bf),
            jax.ShapeDtypeStruct((part, features), bf),
        ],
        scratch_shapes=[pltpu.VMEM((part, rows), bf)],
        compiler_params=pltpu.CompilerParams(vmem_limit_bytes=48 * 2**20),
        cost_estimate=pl.CostEstimate(
            flops=6 * rows * features * part,
            bytes_accessed=4 * rows * features + 6 * rows * part + 6 * features * part,
            transcendentals=0,
        ),
        name="ffn_sums",
    )(n2, seed, hid, dgate, dup)


def reduce_rows(same, other, beside=(), after=()):
    count = lax.axis_size("near") * lax.axis_size("ctx")
    arrived = mate(other.astype(jnp.bfloat16), 1)
    arrived, *after = lax.optimization_barrier((arrived, *after))
    total = same + arrived.astype(jnp.float32)
    blocks = total.reshape(count // 2, -1, total.shape[-1])
    sent = blocks.astype(jnp.bfloat16)
    result, *beside = lax.optimization_barrier((blocks[0], *beside))
    for k in range(1, count // 2):
        result = result + mate(sent[k], 2 * k).astype(jnp.float32)
    return (result, *beside, *after) if beside or after else result


def flipped(values):
    me = lax.axis_index("ctx")
    count = lax.axis_size("ctx")
    bit = 1
    while bit < count:
        v = values.reshape(values.shape[0], count // (2 * bit), 2, bit, *values.shape[2:])
        swapped = jnp.concatenate([v[:, :, 1:], v[:, :, :1]], axis=2)
        values = jnp.where((me & bit) != 0, swapped, v).reshape(values.shape)
        bit *= 2
    return values


def in_order(blocks):
    count = blocks.shape[0]
    me = lax.axis_index("near") * lax.axis_size("ctx") + lax.axis_index("ctx")
    bit = 1
    while bit < count:
        v = blocks.reshape(count // (2 * bit), 2, bit, *blocks.shape[1:])
        swapped = jnp.concatenate([v[:, 1:], v[:, :1]], axis=1)
        blocks = jnp.where((me & bit) != 0, swapped, v).reshape(blocks.shape)
        bit *= 2
    return blocks


def dot(a, b):
    return jnp.dot(a, b, preferred_element_type=jnp.float32)


def across(a, b):
    return lax.dot_general(a, b, (((0,), (0,)), ((), ())), preferred_element_type=jnp.float32)


def against(a, b):
    return lax.dot_general(a, b, (((1,), (1,)), ((), ())), preferred_element_type=jnp.float32)


def scale_rows(values):
    return lax.rsqrt(jnp.mean(values * values, axis=-1, keepdims=True) + EPS)


def norm_back(grad_normed, normed, inverse):
    return inverse * (grad_normed - normed * jnp.mean(grad_normed * normed, axis=-1, keepdims=True))


def on_device(
    tokens,
    segments,
    norm_gain,
    in_weight,
    conv_taps,
    out_weight,
    ffn_gain,
    gate_weight,
    up_weight,
    down_weight,
    cotangent,
):
    seq_count, seq_rows, features = tokens.shape
    rows = seq_count * seq_rows
    n_far = lax.axis_size("far")
    n_near = lax.axis_size("near")
    n_ctx = lax.axis_size("ctx")
    members = n_near * n_ctx
    own = in_weight.shape[0]
    own_ff = down_weight.shape[0]
    part = features // members
    part_ff = n_far * own_ff
    bf, f32 = jnp.bfloat16, jnp.float32
    gain_two = ffn_gain.astype(f32)[:, None]

    everyone = ("far",) + PLANE
    total = n_far * members
    own_tokens = tokens.reshape(rows, features)
    seed_rows = cotangent.reshape(rows, features)

    small = jnp.zeros((16, 128), bf)
    small = small.at[0, :own].set(norm_gain)
    small = small.at[8 : 8 + rows // 128, :].set(segments.reshape(rows // 128, 128).astype(bf))
    small = jnp.broadcast_to(small[None], (total, 16, 128))
    small = lax.all_to_all(small, everyone, split_axis=0, concat_axis=0, tiled=True)
    gain_row = small[:, 0, :own].reshape(features).astype(f32)
    seg_all = lax.dynamic_slice_in_dim(small, lax.axis_index("far") * members, members, axis=0)
    seg_all = seg_all[:, 8 : 8 + rows // 128].reshape(members, rows)
    in_cut = in_weight.reshape(own, 3, total, own).transpose(2, 0, 1, 3)
    in_cut = in_cut.reshape(n_far, members, own, 3, own).transpose(1, 2, 3, 0, 4)
    in_cut = in_cut.reshape(1, members, own, 3 * part)
    in_cut = jnp.broadcast_to(in_cut, (n_far, members, own, 3 * part))
    in_cut = in_cut.reshape(total, own, 3 * part)
    in_cut = lax.all_to_all(in_cut, everyone, split_axis=0, concat_axis=0, tiled=True)
    w_in = in_cut.reshape(features, 3 * part)
    tap_rows = jnp.pad(conv_taps, ((0, 13), (0, features - own)))
    lower = jnp.concatenate([down_weight, out_weight, tap_rows], axis=0)
    lower = lax.all_gather(lower, "far", axis=0, tiled=False)
    w_down = lower[:, :own_ff].reshape(part_ff, features)
    w_out = lower[:, own_ff : own_ff + own].reshape(part, features)
    taps = lower[:, own_ff + own : own_ff + own + 3, :own].astype(f32)
    taps = taps.transpose(1, 0, 2).reshape(3, part)

    def cut_ff(weight):
        scaled = (weight.astype(f32) * gain_two).astype(bf)
        cut = scaled.reshape(own, n_far, members, own_ff).transpose(2, 0, 1, 3)
        return cut.reshape(members, own, part_ff)

    gu_cut = jnp.stack([cut_ff(gate_weight), cut_ff(up_weight)], axis=1)
    gu_cut = lax.all_to_all(gu_cut, PLANE, split_axis=0, concat_axis=0, tiled=True)
    gu_rows = gu_cut.transpose(1, 0, 2, 3).reshape(2, members * own, part_ff)
    gu_all = lax.all_gather(gu_rows, "far", axis=0, tiled=False)
    w_gate = gu_all[:, 0].reshape(features, part_ff)
    w_up = gu_all[:, 1].reshape(features, part_ff)

    seg_true = seg_all.reshape(n_near, n_ctx, seq_count, seq_rows).transpose(0, 2, 1, 3)
    me_near = lax.axis_index("near")
    seg_true = jnp.where(me_near == 0, seg_true, seg_true[::-1])
    length = n_ctx * seq_rows
    seg_true = seg_true.reshape(n_near * seq_count, length)
    outside = jnp.full((n_near * seq_count, 2), -1, bf)
    seg_ext = jnp.concatenate([outside, seg_true], axis=1)
    keep1 = (seg_ext[:, 1 : length + 1] == seg_true).astype(f32)[:, :, None]
    keep2 = (seg_ext[:, :length] == seg_true).astype(f32)[:, :, None]

    def to_true(same, other):
        v = jnp.stack(
            [
                same.reshape(n_near, n_ctx // 2, seq_count, seq_rows, -1),
                other.reshape(n_near, n_ctx // 2, seq_count, seq_rows, -1),
            ],
            axis=2,
        )
        v = flipped(v.reshape(n_near, n_ctx, seq_count, seq_rows, -1))
        return v.transpose(0, 2, 1, 3, 4).reshape(n_near * seq_count, length, -1)

    def to_relative(v):
        v = v.reshape(n_near, seq_count, n_ctx, seq_rows, -1).transpose(0, 2, 1, 3, 4)
        v = flipped(v).reshape(n_near, n_ctx // 2, 2, seq_count, seq_rows, -1)
        half = members // 2 * rows
        return v[:, :, 0].reshape(half, -1), v[:, :, 1].reshape(half, -1)

    def shifted(v, steps):
        fill = jnp.zeros((v.shape[0], abs(steps), v.shape[2]), v.dtype)
        if steps > 0:
            return jnp.concatenate([fill, v[:, :-steps]], axis=1)
        return jnp.concatenate([v[:, -steps:], fill], axis=1)

    def normalized(t):
        v = t.astype(f32)
        return (v * scale_rows(v) * gain_row).astype(bf)

    def summed(left, right):
        return across(left[0], right[0]) + across(left[1], right[1])

    x_all = collect(own_tokens)
    x_all, seed_rows = lax.optimization_barrier((x_all, seed_rows))
    seed_all = collect(seed_rows)
    w_in, seed_all = lax.optimization_barrier((w_in, seed_all))
    x_all = halves(x_all)
    h_in = tuple(normalized(t) for t in x_all)
    proj = [dot(n, w_in) for n in h_in]
    part_b = [p[:, :part] for p in proj]
    part_c = [p[:, part : 2 * part] for p in proj]
    part_x = [p[:, 2 * part :] for p in proj]
    mixed_in = to_true(*[(b * x).astype(bf) for b, x in zip(part_b, part_x)]).astype(f32)
    previous = shifted(mixed_in, 1) * keep1
    earlier = shifted(mixed_in, 2) * keep2
    short = to_relative(taps[2] * mixed_in + taps[1] * previous + taps[0] * earlier)
    gated = [(c * s).astype(bf) for c, s in zip(part_c, short)]
    branch = reduce_rows(*[dot(g, w_out) for g in gated])
    resid = own_tokens.astype(f32) + branch
    inverse2 = scale_rows(resid)
    normed2 = resid * inverse2

    n2_all = collect(normed2.astype(bf))
    n2_all, seed_all, hidden, d_gate, d_up, part_mixed, d_same, d_other = ffn(
        n2_all, seed_all, w_gate, w_up, w_down
    )
    sum_gate, sum_up, sum_down = weight_sums(n2_all, seed_all, hidden, d_gate, d_up)
    sum_down = sum_down.reshape(n_far, own_ff, features)
    d_n2, sum_gate, sum_up, sum_down = reduce_rows(
        d_same, d_other, beside=(sum_gate, sum_up, sum_down)
    )
    own_gu = jnp.stack(
        [
            lax.psum_scatter(sum_gate, "far", scatter_dimension=0, tiled=True),
            lax.psum_scatter(sum_up, "far", scatter_dimension=0, tiled=True),
        ]
    )
    d_resid = seed_rows.astype(f32) + norm_back(d_n2, normed2, inverse2)

    d_branch = collect(d_resid.astype(bf))
    d_branch = halves(d_branch)
    d_branch, part_mixed = lax.optimization_barrier((d_branch, part_mixed))
    mixed = (resid + reduce_rows(*[m.astype(f32) for m in jnp.split(part_mixed, 2)])).astype(bf)
    d_gated = [against(d, w_out) for d in d_branch]
    d_short = to_true(*[(d * c).astype(bf) for d, c in zip(d_gated, part_c)]).astype(f32)
    sum_taps = jnp.stack(
        [
            jnp.sum(d_short * earlier, axis=(0, 1)),
            jnp.sum(d_short * previous, axis=(0, 1)),
            jnp.sum(d_short * mixed_in, axis=(0, 1)),
        ]
    )
    d_mixed = to_relative(
        taps[2] * d_short
        + shifted(taps[1] * keep1 * d_short, -1)
        + shifted(taps[0] * keep2 * d_short, -2)
    )
    d_proj = [
        jnp.concatenate([dm * x, dg * s, dm * b], axis=1).astype(bf)
        for dm, dg, s, b, x in zip(d_mixed, d_gated, short, part_b, part_x)
    ]
    sum_in = summed(h_in, d_proj).astype(bf).reshape(total, own, 3 * part)
    d_proj, sum_in = lax.optimization_barrier((d_proj, sum_in))
    d_n1 = reduce_rows(*[against(d, w_in) for d in d_proj]) * gain_row
    values = own_tokens.astype(f32)
    inverse1 = scale_rows(values)
    input_grad = d_resid + norm_back(d_n1, values * inverse1, inverse1)

    own_in = lax.all_to_all(sum_in, everyone, split_axis=0, concat_axis=0, tiled=True)
    own_in = own_in.reshape(n_far, members, own, 3 * part).astype(f32).sum(axis=0)
    own_in = own_in.reshape(members, own, 3, n_far, own).transpose(1, 2, 3, 0, 4)
    grad_in = own_in.reshape(own, 3 * features)
    grad_gain1 = jnp.sum(in_weight.astype(f32) * grad_in, axis=1) / norm_gain.astype(f32)
    sum_out = summed(gated, d_branch).astype(bf).reshape(n_far, own, features)
    tap_sums = sum_taps.astype(bf).reshape(3, n_far, own).transpose(1, 0, 2)
    tap_sums = jnp.pad(tap_sums, ((0, 0), (0, 13), (0, features - own)))
    lower_sum = jnp.concatenate([sum_down, sum_out, tap_sums], axis=1)
    own_gu = own_gu.reshape(2, members, own, part_ff).transpose(1, 0, 2, 3)
    own_gu = lax.all_to_all(own_gu, PLANE, split_axis=0, concat_axis=0, tiled=True)
    own_lower = lax.psum_scatter(lower_sum, "far", scatter_dimension=0, tiled=False)
    own_lower = own_lower.astype(f32)
    grad_out = own_lower[own_ff : own_ff + own]
    grad_taps = own_lower[own_ff + own : own_ff + own + 3, :own]
    own_gu = own_gu.reshape(members, 2, own, n_far, own_ff).transpose(1, 2, 3, 0, 4)
    own_gu = own_gu.reshape(2, own, members * part_ff).astype(f32)
    grad_gate = own_gu[0] * gain_two
    grad_up = own_gu[1] * gain_two
    grad_gain2 = jnp.sum(
        gate_weight.astype(f32) * own_gu[0] + up_weight.astype(f32) * own_gu[1], axis=1
    )
    return (
        mixed.reshape(seq_count, seq_rows, features),
        input_grad.reshape(seq_count, seq_rows, features),
        grad_gain1,
        grad_in,
        grad_taps,
        grad_out,
        grad_gain2,
        grad_gate,
        grad_up,
        own_lower[:own_ff],
    )


def solution(mesh):
    dp, ctx = mesh.shape["dp"], mesh.shape["ctx"]
    near = 2 if dp % 2 == 0 else 1
    fine = Mesh(mesh.devices.reshape(dp // near, near, ctx), ("far", "near", "ctx"))
    seq = ("far", "near")
    every = ("far", "near", "ctx")
    in_specs = (
        P(seq, "ctx", None),
        P(seq, "ctx"),
        P(every),
        P(every, None),
        P(None, every),
        P(every, None),
        P(every),
        P(every, None),
        P(every, None),
        P(every, None),
        P(seq, "ctx", None),
    )
    out_specs = (
        P(seq, "ctx", None),
        P(seq, "ctx", None),
        P(every),
        P(every, None),
        P(None, every),
        P(every, None),
        P(every),
        P(every, None),
        P(every, None),
        P(every, None),
    )
    return jax.shard_map(
        on_device, mesh=fine, in_specs=in_specs, out_specs=out_specs, check_vma=False
    )
```

time: 915 us -> 291 us (0.32)
  waiting for transfers between devices: 627 us -> 98.3 us
  blocking collectives: 134 us -> 0 us
  matrix products: 77.4 us -> 13.9 us
  local copies, waits for them, and re-layouts: 20 us -> 48.6 us
  starting transfers between devices: 27.3 us -> 55.3 us
  Pallas kernels: 0 us -> 27 us
  other arithmetic: 13.4 us -> 30.9 us
    all_gather x10 -> x2, waiting for transfers between devices: 294 us -> 0.02 us  [the longest x1 0.02 us: on_device(): lower = lax.all_gather(lower, 'far', axis=0, tiled=False)]
    reduce_scatter x3, waiting for transfers between devices: 245 us -> 0.01 us  [the longest x1 0.01 us: on_device(): lax.psum_scatter(sum_gate, 'far', scatter_dimension=0, tiled=True)]
    ppermute x3 -> x44, waiting for transfers between devices: 2.41 us -> 81.2 us  [mate(): return lax.ppermute(value, PLANE, [(k, k ^ flip) for k in range(count)])]
    all_to_all x5, waiting for transfers between devices: 81.2 us -> 17 us  [the longest x1 8.8 us: on_device(): lax.all_to_all(gu_cut, PLANE, split_axis=0, concat_axis=0, tiled=True)]
    dot_general x15 -> x12, matrix products: 77.4 us -> 13.9 us  [the longest x4 5.48 us: across(): lax.dot_general(a, b, (((0,), (0,)), ((), ())), preferred_element_type=jn...]
    unnamed x2 -> x0, blocking collectives: 52.4 us -> none
    all_gather x1 -> x0, blocking collectives: 40.9 us -> none  [on_device(): lax.all_gather(conv_taps, ('dp', 'ctx'), axis=1, tiled=True)]
    all_to_all x2 -> x0, blocking collectives: 40.8 us -> none  [the longest x1 29.6 us: on_device(): lax.all_to_all(by_owner(hidden, dp_count, ctx_count), 'ctx', split_axis=2...]
  transfers between devices with their start and end apart: 22 -> 54, of which waited for: 16 -> 28; matrix products, arithmetic and copies ran while one was open for 12% -> 27% of each run, Pallas kernels for 0% -> 3%
where the time goes in v1:
time: 291 us; the launch traced here: 289 us
  waiting for transfers between devices  98.3 us (34%)
  starting transfers between devices  55.3 us (19%)
  local copies, waits for them, and re-layouts  48.6 us (17%)
  other arithmetic  30.9 us (11%)
  Pallas kernels  27 us (9%)
  between operations  15.3 us (5%)
  matrix products  13.9 us (5%)
    ppermute x44, waiting for transfers between devices, mate(): return lax.ppermute(value, PLANE, [(k, k ^ flip) for k in range(count)])  81.2 us
    ppermute x44, starting transfers between devices, mate(): return lax.ppermute(value, PLANE, [(k, k ^ flip) for k in range(count)])  31.3 us
    pallas_call x1, Pallas kernels, ffn(): pl.pallas_call(functools.partial(ffn_rows, steps, count), grid=(steps,),...  18.4 us
    unnamed x163, local copies, waits for them, and re-layouts  9.91 us
    all_to_all x1, waiting for transfers between devices, on_device(): lax.all_to_all(gu_cut, PLANE, split_axis=0, concat_axis=0, tiled=True)  8.8 us
    pallas_call x1, Pallas kernels, weight_sums(): pl.pallas_call(ffn_sums, grid=(4,), in_specs=[column(rows), column(rows),...  8.59 us
    all_to_all x1, starting transfers between devices, on_device(): lax.all_to_all(small, everyone, split_axis=0, concat_axis=0, tiled=True)  7.3 us
  transfers between devices with their start and end apart: 54, of which 28 were waited for; matrix products, arithmetic and copies ran while one was open for 27% of the time, Pallas kernels for 3%

profile of v1, /device:TPU:0, one launch (start us, length us, event | category | flops | bytes accessed | tf_op | source)
XLA Modules:
  0.0 289.3 jit_solution(5014228182882427592)
XLA Ops:
  9.3 7.3 %all-to-all-start = ((bf16[32,16,128]{2,1,0:T(8,128)(2,1)}), bf16[32,16,128]{2,1,0:T(8,128)(2,1)S(1)}, u32[]{:S(2)}, u32[]{:S(2)}) async-start(bf16[32,16,128]{2,1,0:T(8,128)(2,1)} %broadcast_in_dim.6), calls=%async_computation | async-start | bytes 262144 | tf_op jit(solution)/shard_map/all_to_all | solution.py:256
  16.7 1.8 fusion.20
  25.5 3.5 %all-to-all-start.2 = ((bf16[8,2,32,576]{3,2,1,0:T(8,128)(2,1)}), bf16[8,2,32,576]{3,2,1,0:T(8,128)(2,1)S(1)}, u32[]{:S(2)}, u32[]{:S(2)}) async-start(bf16[8,2,32,576]{3,2,1,0:T(8,128)(2,1)} %copy.257), calls=%async_computation.2 | async-start | bytes 1310720 | tf_op jit(solution)/shard_map/all_to_all | solution.py:281
  30.4 8.8 %all-to-all-done.2 = bf16[8,2,32,576]{3,2,1,0:T(8,128)(2,1)S(1)} async-done(((bf16[8,2,32,576]{3,2,1,0:T(8,128)(2,1)}), bf16[8,2,32,576]{3,2,1,0:T(8,128)(2,1)S(1)}, u32[]{:S(2)}, u32[]{:S(2)}) %all-to-all-start.2) | async-done | bytes 589856 | tf_op jit(solution)/shard_map/all_to_all | solution.py:281
  40.3 4.5 %all-to-all-start.1 = ((bf16[32,32,384]{2,1,0:T(8,128)(2,1)}), bf16[32,32,384]{2,1,0:T(8,128)(2,1)S(1)}, u32[]{:S(2)}, u32[]{:S(2)}) async-start(bf16[32,32,384]{2,1,0:T(8,128)(2,1)} %bitcast.7), calls=%async_computation.1 | async-start | bytes 1572864 | tf_op jit(solution)/shard_map/all_to_all | solution.py:265
  44.9 1.8 collective-permute-start
  49.3 8.6 %collective-permute-done = bf16[128,1024]{1,0:T(8,128)(2,1)S(1)} collective-permute-done((bf16[128,1024]{1,0:T(8,128)(2,1)S(1)}, bf16[128,1024]{1,0:T(8,128)(2,1)S(1)}, u32[]{:S(2)}, u32[]{:S(2)}) %collective-permute-start) | collective-permute-done | bytes 262176 | tf_op jit(solution)/shard_map/ppermute | solution.py:17
  58.7 8.0 %collective-permute-done.2 = bf16[128,1024]{1,0:T(8,128)(2,1)S(1)} collective-permute-done((bf16[128,1024]{1,0:T(8,128)(2,1)S(1)}, bf16[128,1024]{1,0:T(8,128)(2,1)S(1)}, u32[]{:S(2)}, u32[]{:S(2)}) %collective-permute-start.2) | collective-permute-done | bytes 262176 | tf_op jit(solution)/shard_map/ppermute | solution.py:17
  69.3 2.5 collective-permute-start.9
  75.3 1.8 fusion.1
  78.7 5.6 %collective-permute-done.9.refs_11_ = bf16[128,1024]{1,0:T(8,128)(2,1)S(1)} collective-permute-done((bf16[128,1024]{1,0:T(8,128)(2,1)S(1)}, bf16[128,1024]{1,0:T(8,128)(2,1)S(1)}, u32[]{:S(2)}, u32[]{:S(2)}) %collective-permute-start.9) | collective-permute-done | bytes 262176 | tf_op jit(solution)/shard_map/ppermute | solution.py:17
  84.4 1.5 collective-permute-done.13.refs_15_
  85.9 2.1 fusion.26
  100.5 2.6 collective-permute-start.17
  103.1 4.9 %collective-permute-done.15 = bf16[128,1024]{1,0:T(8,128)(2,1)S(1)} collective-permute-done((bf16[128,1024]{1,0:T(8,128)(2,1)S(1)}, bf16[128,1024]{1,0:T(8,128)(2,1)S(1)}, u32[]{:S(2)}, u32[]{:S(2)}) %collective-permute-start.15) | collective-permute-done | bytes 262176 | tf_op jit(solution)/shard_map/ppermute | solution.py:17
  109.3 5.5 %collective-permute-done.17 = bf16[128,1024]{1,0:T(8,128)(2,1)S(1)} collective-permute-done((bf16[128,1024]{1,0:T(8,128)(2,1)S(1)}, bf16[128,1024]{1,0:T(8,128)(2,1)S(1)}, u32[]{:S(2)}, u32[]{:S(2)}) %collective-permute-start.17) | collective-permute-done | bytes 262176 | tf_op jit(solution)/shard_map/ppermute | solution.py:17
  116.8 2.6 collective-permute-start.20
  120.5 3.7 %collective-permute-done.18.refs_1_ = bf16[128,1024]{1,0:T(8,128)(2,1)S(1)} collective-permute-done((bf16[128,1024]{1,0:T(8,128)(2,1)S(1)}, bf16[128,1024]{1,0:T(8,128)(2,1)S(1)}, u32[]{:S(2)}, u32[]{:S(2)}) %collective-permute-start.18) | collective-permute-done | bytes 262176 | tf_op jit(solution)/shard_map/ppermute | solution.py:17
  125.7 4.4 %collective-permute-done.20.refs_3_ = bf16[128,1024]{1,0:T(8,128)(2,1)S(1)} collective-permute-done((bf16[128,1024]{1,0:T(8,128)(2,1)S(1)}, bf16[128,1024]{1,0:T(8,128)(2,1)S(1)}, u32[]{:S(2)}, u32[]{:S(2)}) %collective-permute-start.20) | collective-permute-done | bytes 262176 | tf_op jit(solution)/shard_map/ppermute | solution.py:17
  130.1 3.2 %fusion.44 = (bf16[4,1,256,576]{2,3,1,0:T(8,128)(2,1)}, bf16[4,1,256,576]{2,3,1,0:T(8,128)(2,1)}) fusion(bf16[4,2,256,576]{2,3,1,0:T(8,128)(2,1)} %all-gather.4.cloned.1.call-done), kind=kLoop, calls=%fused_computation.151 | loop fusion | bytes 4718592 | tf_op jit(solution)/shard_map/slice | solution.py:285
  133.3 2.4 copy.260
  135.7 2.4 copy.261
  138.2 18.4 %ffn_rows.1 = (bf16[1024,1024]{1,0:T(8,128)(2,1)}, bf16[1024,1024]{1,0:T(8,128)(2,1)}, bf16[1024,576]{1,0:T(8,128)(2,1)}, bf16[1024,576]{1,0:T(8,128)(2,1)}, bf1...) custom-call(bf16[128,1024]{1,0:T(8,128)(2,1)S(1)} %multiply_convert_fu, ...), custom_call_target="tpu_custom_call" | custom-call | flops 7247757312 | bytes 21757952 | tf_op jit(solution)/shard_map/ffn_rows/pallas_call | solution.py:97
  158.4 8.6 %ffn_sums.1 = (bf16[1024,576]{1,0:T(8,128)(2,1)}, bf16[1024,576]{1,0:T(8,128)(2,1)}, bf16[576,1024]{1,0:T(8,128)(2,1)S(1)}) custom-call(bf16[1024,1024]{1,0:T(8,128)(2,1)} %get-tuple-element.93.n2, bf16[1024,1024]{1,0:T(8,128)(2,1)} %get-tuple-element.94.seed, bf16[1024,576]{1,0:T(8,128)(2,1)S(1)} %copy-done.1, bf16[1024,576]{1,0:T(8,128)(2,1)} %get-tuple-element.96.dgate, ...), custom_call_target="tpu_custom_call" | custom-call | flops 3623878656 | bytes 11272192 | tf_op jit(solution)/shard_map/ffn_sums/pallas_call | solution.py:139
  170.9 2.6 collective-permute-start.28
  173.5 4.8 %collective-permute-done.26 = bf16[128,1024]{1,0:T(8,128)(2,1)S(1)} collective-permute-done((bf16[128,1024]{1,0:T(8,128)(2,1)S(1)}, bf16[128,1024]{1,0:T(8,128)(2,1)S(1)}, u32[]{:S(2)}, u32[]{:S(2)}) %collective-permute-start.26) | collective-permute-done | bytes 262176 | tf_op jit(solution)/shard_map/ppermute | solution.py:17
  179.8 5.3 %collective-permute-done.28 = bf16[128,1024]{1,0:T(8,128)(2,1)S(1)} collective-permute-done((bf16[128,1024]{1,0:T(8,128)(2,1)S(1)}, bf16[128,1024]{1,0:T(8,128)(2,1)S(1)}, u32[]{:S(2)}, u32[]{:S(2)}) %collective-permute-start.28) | collective-permute-done | bytes 262176 | tf_op jit(solution)/shard_map/ppermute | solution.py:17
  187.2 2.6 collective-permute-start.31
  189.8 5.0 %collective-permute-done.29 = bf16[128,1024]{1,0:T(8,128)(2,1)} collective-permute-done((bf16[128,1024]{1,0:T(8,128)(2,1)S(1)}, bf16[128,1024]{1,0:T(8,128)(2,1)}, u32[]{:S(2)}, u32[]{:S(2)}) %collective-permute-start.29) | collective-permute-done | bytes 262176 | tf_op jit(solution)/shard_map/ppermute | solution.py:17
  196.2 4.2 %collective-permute-done.31 = bf16[128,1024]{1,0:T(8,128)(2,1)} collective-permute-done((bf16[128,1024]{1,0:T(8,128)(2,1)S(1)}, bf16[128,1024]{1,0:T(8,128)(2,1)}, u32[]{:S(2)}, u32[]{:S(2)}) %collective-permute-start.31) | collective-permute-done | bytes 262176 | tf_op jit(solution)/shard_map/ppermute | solution.py:17
  210.7 1.8 add_convert_fusion
  212.5 1.8 convolution_convert_fusion.1
  218.0 2.3 split.7
  221.7 3.6 %all-to-all-start.3 = ((bf16[32,32,384]{2,1,0:T(8,128)(2,1)}), bf16[32,32,384]{2,1,0:T(8,128)(2,1)}, u32[]{:S(2)}, u32[]{:S(2)}) async-start(bf16[32,32,384]{2,1,0:T(8,128)(2,1)} %bitcast.276), calls=%async_computation.3 | async-start | bytes 1572864 | tf_op jit(solution)/shard_map/all_to_all | solution.py:393
  225.4 1.7 fusion.8
  228.6 2.1 fusion.58
  230.8 1.8 collective-permute-start.41
  234.3 1.7 convert_add_fusion.1
  236.1 1.8 collective-permute-start.37
  239.4 3.4 %collective-permute-done.41 = bf16[128,1024]{1,0:T(8,128)(2,1)S(1)} collective-permute-done((bf16[128,1024]{1,0:T(8,128)(2,1)S(1)}, bf16[128,1024]{1,0:T(8,128)(2,1)S(1)}, u32[]{:S(2)}, u32[]{:S(2)}) %collective-permute-start.41) | collective-permute-done | bytes 262176 | tf_op jit(solution)/shard_map/ppermute | solution.py:17
  242.8 1.9 collective-permute-start.39
  244.7 6.5 %collective-permute-done.43 = bf16[128,1024]{1,0:T(8,128)(2,1)S(1)} collective-permute-done((bf16[128,1024]{1,0:T(8,128)(2,1)S(1)}, bf16[128,1024]{1,0:T(8,128)(2,1)S(1)}, u32[]{:S(2)}, u32[]{:S(2)}) %collective-permute-start.43) | collective-permute-done | bytes 262176 | tf_op jit(solution)/shard_map/ppermute | solution.py:17
  252.6 2.0 maximum_bitcast_fusion
  254.6 3.1 %all-to-all-done.3 = bf16[32,32,384]{2,1,0:T(8,128)(2,1)} async-done(((bf16[32,32,384]{2,1,0:T(8,128)(2,1)}), bf16[32,32,384]{2,1,0:T(8,128)(2,1)}, u32[]{:S(2)}, u32[]{:S(2)}) %all-to-all-start.3) | async-done | bytes 786464 | tf_op jit(solution)/shard_map/all_to_all | solution.py:393
  257.7 4.5 %all-to-all-start.4 = ((bf16[8,2,32,576]{3,2,1,0:T(8,128)(2,1)}), bf16[8,2,32,576]{3,2,1,0:T(8,128)(2,1)}, u32[]{:S(2)}, u32[]{:S(2)}) async-start(bf16[8,2,32,576]{3,2,1,0:T(8,128)(2,1)} %maximum_bitcast_fusion), calls=%async_computation.7 | async-start | bytes 1310720 | tf_op jit(solution)/shard_map/all_to_all | solution.py:403
  267.7 4.5 %all-to-all-done.4 = bf16[8,2,32,576]{3,2,1,0:T(8,128)(2,1)} async-done(((bf16[8,2,32,576]{3,2,1,0:T(8,128)(2,1)}), bf16[8,2,32,576]{3,2,1,0:T(8,128)(2,1)}, u32[]{:S(2)}, u32[]{:S(2)}) %all-to-all-start.4) | async-done | bytes 589856 | tf_op jit(solution)/shard_map/all_to_all | solution.py:403
  272.2 2.8 reshape.698
  277.7 1.8 broadcast_multiply_fusion
  (378 shorter events, 84.1 us)
Async XLA Ops:
  9.3 15.5 %all-to-all-start = ((bf16[32,16,128]{2,1,0:T(8,128)(2,1)}), bf16[32,16,128]{2,1,0:T(8,128)(2,1)S(1)}, u32[]{:S(2)}, u32[]{:S(2)}) async-start(bf16[32,16,128]{2,1,0:T(8,128)(2,1)} %broadcast_in_dim.6), calls=%async_computation | async-start | bytes 262144 | tf_op jit(solution)/shard_map/all_to_all | solution.py:256
  16.6 74.3 %all-gather.6.cloned.1.call-start = ((), (), s32[]{:S(2)}) async-start(), calls=%async_computation.12 | async-start | bytes 1966080 | tf_op jit(solution)/shard_map/all_gather | solution.py:269
  25.5 13.7 %all-to-all-start.2 = ((bf16[8,2,32,576]{3,2,1,0:T(8,128)(2,1)}), bf16[8,2,32,576]{3,2,1,0:T(8,128)(2,1)S(1)}, u32[]{:S(2)}, u32[]{:S(2)}) async-start(bf16[8,2,32,576]{3,2,1,0:T(8,128)(2,1)} %copy.257), calls=%async_computation.2 | async-start | bytes 1310720 | tf_op jit(solution)/shard_map/all_to_all | solution.py:281
  40.3 45.6 %all-to-all-start.1 = ((bf16[32,32,384]{2,1,0:T(8,128)(2,1)}), bf16[32,32,384]{2,1,0:T(8,128)(2,1)S(1)}, u32[]{:S(2)}, u32[]{:S(2)}) async-start(bf16[32,32,384]{2,1,0:T(8,128)(2,1)} %bitcast.7), calls=%async_computation.1 | async-start | bytes 1572864 | tf_op jit(solution)/shard_map/all_to_all | solution.py:265
  44.8 85.3 %all-gather.4.cloned.1.call-start = ((), (), s32[]{:S(2)}) async-start(), calls=%async_computation.8 | async-start | bytes 2949120 | tf_op jit(solution)/shard_map/all_gather | solution.py:283
  44.9 12.9 %collective-permute-start = (bf16[128,1024]{1,0:T(8,128)(2,1)S(1)}, bf16[128,1024]{1,0:T(8,128)(2,1)S(1)}, u32[]{:S(2)}, u32[]{:S(2)}) collective-permute-start(bf16[128,1024]{1,0:T(8,128)(2,1)S(1)} %bitcast.223), channel_id=1, source_target_pairs={{0,2},{1,3},{2,0},{3,1},{4,6},{5,7},{6,4},{7,5},{8,10},{9,11},{10,... | collective-permute-start | bytes 786440 | tf_op jit(solution)/shard_map/ppermute | solution.py:17
  46.7 11.9 %collective-permute-start.1 = (bf16[128,1024]{1,0:T(8,128)(2,1)S(1)}, bf16[128,1024]{1,0:T(8,128)(2,1)S(1)}, u32[]{:S(2)}, u32[]{:S(2)}) collective-permute-start(bf16[128,1024]{1,0:T(8,128)(2,1)S(1)} %bitcast.224), channel_id=1, source_target_pairs={{0,4},{1,5},{2,6},{3,7},{4,0},{5,1},{6,2},{7,3},{8,12},{9,13},{10,... | collective-permute-start | bytes 786440 | tf_op jit(solution)/shard_map/ppermute | solution.py:17
  48.2 18.5 %collective-permute-start.2 = (bf16[128,1024]{1,0:T(8,128)(2,1)S(1)}, bf16[128,1024]{1,0:T(8,128)(2,1)S(1)}, u32[]{:S(2)}, u32[]{:S(2)}) collective-permute-start(bf16[128,1024]{1,0:T(8,128)(2,1)S(1)} %bitcast.225), channel_id=1, source_target_pairs={{0,6},{1,7},{2,4},{3,5},{4,2},{5,3},{6,0},{7,1},{8,14},{9,15},{10,... | collective-permute-start | bytes 786440 | tf_op jit(solution)/shard_map/ppermute | solution.py:17
  48.5 18.4 %collective-permute-start.3 = (bf16[128,1024]{1,0:T(8,128)(2,1)S(1)}, bf16[128,1024]{1,0:T(8,128)(2,1)S(1)}, u32[]{:S(2)}, u32[]{:S(2)}) collective-permute-start(bf16[128,1024]{1,0:T(8,128)(2,1)S(1)} %bitcast.226), channel_id=1, source_target_pairs={{0,1},{1,0},{2,3},{3,2},{4,5},{5,4},{6,7},{7,6},{8,9},{9,8},{10,11... | collective-permute-start | bytes 786440 | tf_op jit(solution)/shard_map/ppermute | solution.py:17
  57.8 9.0 %collective-permute-start.4 = (bf16[128,1024]{1,0:T(8,128)(2,1)S(1)}, bf16[128,1024]{1,0:T(8,128)(2,1)S(1)}, u32[]{:S(2)}, u32[]{:S(2)}) collective-permute-start(bf16[128,1024]{1,0:T(8,128)(2,1)S(1)} %collective-permute-done), channel_id=1, source_target_pairs={{0,1},{1,0},{2,3},{3,2},{4,5},{5,4},{6,7},{7,6},{8,9},{9,8},{10,11... | collective-permute-start | bytes 786440 | tf_op jit(solution)/shard_map/ppermute | solution.py:17
  58.7 8.2 %collective-permute-start.5 = (bf16[128,1024]{1,0:T(8,128)(2,1)S(1)}, bf16[128,1024]{1,0:T(8,128)(2,1)S(1)}, u32[]{:S(2)}, u32[]{:S(2)}) collective-permute-start(bf16[128,1024]{1,0:T(8,128)(2,1)S(1)} %collective-permute-done.1), channel_id=1, source_target_pairs={{0,1},{1,0},{2,3},{3,2},{4,5},{5,4},{6,7},{7,6},{8,9},{9,8},{10,11... | collective-permute-start | bytes 786440 | tf_op jit(solution)/shard_map/ppermute | solution.py:17
  68.2 9.8 %collective-permute-start.7 = (bf16[128,1024]{1,0:T(8,128)(2,1)S(1)}, bf16[128,1024]{1,0:T(8,128)(2,1)S(1)}, u32[]{:S(2)}, u32[]{:S(2)}) collective-permute-start(bf16[128,1024]{1,0:T(8,128)(2,1)S(1)} %bitcast.201), channel_id=1, source_target_pairs={{0,2},{1,3},{2,0},{3,1},{4,6},{5,7},{6,4},{7,5},{8,10},{9,11},{10,... | collective-permute-start | bytes 786440 | tf_op jit(solution)/shard_map/ppermute | solution.py:17
  69.0 9.7 %collective-permute-start.8 = (bf16[128,1024]{1,0:T(8,128)(2,1)S(1)}, bf16[128,1024]{1,0:T(8,128)(2,1)S(1)}, u32[]{:S(2)}, u32[]{:S(2)}) collective-permute-start(bf16[128,1024]{1,0:T(8,128)(2,1)S(1)} %bitcast.202), channel_id=1, source_target_pairs={{0,4},{1,5},{2,6},{3,7},{4,0},{5,1},{6,2},{7,3},{8,12},{9,13},{10,... | collective-permute-start | bytes 786440 | tf_op jit(solution)/shard_map/ppermute | solution.py:17
  69.3 15.0 %collective-permute-start.9 = (bf16[128,1024]{1,0:T(8,128)(2,1)S(1)}, bf16[128,1024]{1,0:T(8,128)(2,1)S(1)}, u32[]{:S(2)}, u32[]{:S(2)}) collective-permute-start(bf16[128,1024]{1,0:T(8,128)(2,1)S(1)} %bitcast.203), channel_id=1, source_target_pairs={{0,6},{1,7},{2,4},{3,5},{4,2},{5,3},{6,0},{7,1},{8,14},{9,15},{10,... | collective-permute-start | bytes 786440 | tf_op jit(solution)/shard_map/ppermute | solution.py:17
  75.0 177.6 %reduce-scatter.6.cloned.1.call-start = ((), (), s32[]{:S(2)}) async-start(), calls=%async_computation.10 | async-start | bytes 1638400 | tf_op jit(solution)/shard_map/reduce_scatter | solution.py:358
  75.2 9.1 %collective-permute-start.10 = (bf16[128,1024]{1,0:T(8,128)(2,1)S(1)}, bf16[128,1024]{1,0:T(8,128)(2,1)S(1)}, u32[]{:S(2)}, u32[]{:S(2)}) collective-permute-start(bf16[128,1024]{1,0:T(8,128)(2,1)S(1)} %bitcast.204), channel_id=1, source_target_pairs={{0,1},{1,0},{2,3},{3,2},{4,5},{5,4},{6,7},{7,6},{8,9},{9,8},{10,11... | collective-permute-start | bytes 786440 | tf_op jit(solution)/shard_map/ppermute | solution.py:17
  78.1 6.3 %collective-permute-start.11 = (bf16[128,1024]{1,0:T(8,128)(2,1)S(1)}, bf16[128,1024]{1,0:T(8,128)(2,1)S(1)}, u32[]{:S(2)}, u32[]{:S(2)}) collective-permute-start(bf16[128,1024]{1,0:T(8,128)(2,1)S(1)} %collective-permute-done.7.refs_9_), channel_id=1, source_target_pairs={{0,1},{1,0},{2,3},{3,2},{4,5},{5,4},{6,7},{7,6},{8,9},{9,8},{10,11... | collective-permute-start | bytes 786440 | tf_op jit(solution)/shard_map/ppermute | solution.py:17
  99.5 8.5 %collective-permute-start.15 = (bf16[128,1024]{1,0:T(8,128)(2,1)S(1)}, bf16[128,1024]{1,0:T(8,128)(2,1)S(1)}, u32[]{:S(2)}, u32[]{:S(2)}) collective-permute-start(bf16[128,1024]{1,0:T(8,128)(2,1)S(1)} %get-tuple-element.143), channel_id=1, source_target_pairs={{0,2},{1,3},{2,0},{3,1},{4,6},{5,7},{6,4},{7,5},{8,10},{9,11},{10,... | collective-permute-start | bytes 786440 | tf_op jit(solution)/shard_map/ppermute | solution.py:17
  100.1 9.2 %collective-permute-start.16 = (bf16[128,1024]{1,0:T(8,128)(2,1)S(1)}, bf16[128,1024]{1,0:T(8,128)(2,1)S(1)}, u32[]{:S(2)}, u32[]{:S(2)}) collective-permute-start(bf16[128,1024]{1,0:T(8,128)(2,1)S(1)} %get-tuple-element.145), channel_id=1, source_target_pairs={{0,4},{1,5},{2,6},{3,7},{4,0},{5,1},{6,2},{7,3},{8,12},{9,13},{10,... | collective-permute-start | bytes 786440 | tf_op jit(solution)/shard_map/ppermute | solution.py:17
  100.5 14.3 %collective-permute-start.17 = (bf16[128,1024]{1,0:T(8,128)(2,1)S(1)}, bf16[128,1024]{1,0:T(8,128)(2,1)S(1)}, u32[]{:S(2)}, u32[]{:S(2)}) collective-permute-start(bf16[128,1024]{1,0:T(8,128)(2,1)S(1)} %get-tuple-element.144), channel_id=1, source_target_pairs={{0,6},{1,7},{2,4},{3,5},{4,2},{5,3},{6,0},{7,1},{8,14},{9,15},{10,... | collective-permute-start | bytes 786440 | tf_op jit(solution)/shard_map/ppermute | solution.py:17
  115.8 8.4 %collective-permute-start.18 = (bf16[128,1024]{1,0:T(8,128)(2,1)S(1)}, bf16[128,1024]{1,0:T(8,128)(2,1)S(1)}, u32[]{:S(2)}, u32[]{:S(2)}) collective-permute-start(bf16[128,1024]{1,0:T(8,128)(2,1)S(1)} %multiply_convert_fusion.refs_0_), channel_id=1, source_target_pairs={{0,2},{1,3},{2,0},{3,1},{4,6},{5,7},{6,4},{7,5},{8,10},{9,11},{10,... | collective-permute-start | bytes 786440 | tf_op jit(solution)/shard_map/ppermute | solution.py:17
  116.4 9.2 %collective-permute-start.19 = (bf16[128,1024]{1,0:T(8,128)(2,1)S(1)}, bf16[128,1024]{1,0:T(8,128)(2,1)S(1)}, u32[]{:S(2)}, u32[]{:S(2)}) collective-permute-start(bf16[128,1024]{1,0:T(8,128)(2,1)S(1)} %multiply_convert_fusion.refs_0_), channel_id=1, source_target_pairs={{0,4},{1,5},{2,6},{3,7},{4,0},{5,1},{6,2},{7,3},{8,12},{9,13},{10,... | collective-permute-start | bytes 786440 | tf_op jit(solution)/shard_map/ppermute | solution.py:17
  116.8 13.3 %collective-permute-start.20 = (bf16[128,1024]{1,0:T(8,128)(2,1)S(1)}, bf16[128,1024]{1,0:T(8,128)(2,1)S(1)}, u32[]{:S(2)}, u32[]{:S(2)}) collective-permute-start(bf16[128,1024]{1,0:T(8,128)(2,1)S(1)} %multiply_convert_fusion.refs_0_), channel_id=1, source_target_pairs={{0,6},{1,7},{2,4},{3,5},{4,2},{5,3},{6,0},{7,1},{8,14},{9,15},{10,... | collective-permute-start | bytes 786440 | tf_op jit(solution)/shard_map/ppermute | solution.py:17
  120.5 17.7 %collective-permute-start.21 = (bf16[128,1024]{1,0:T(8,128)(2,1)S(1)}, bf16[128,1024]{1,0:T(8,128)(2,1)S(1)}, u32[]{:S(2)}, u32[]{:S(2)}) collective-permute-start(bf16[128,1024]{1,0:T(8,128)(2,1)S(1)} %multiply_convert_fusion.refs_0_), channel_id=1, source_target_pairs={{0,1},{1,0},{2,3},{3,2},{4,5},{5,4},{6,7},{7,6},{8,9},{9,8},{10,11... | collective-permute-start | bytes 786440 | tf_op jit(solution)/shard_map/ppermute | solution.py:17
  124.2 14.0 %collective-permute-start.22 = (bf16[128,1024]{1,0:T(8,128)(2,1)S(1)}, bf16[128,1024]{1,0:T(8,128)(2,1)}, u32[]{:S(2)}, u32[]{:S(2)}) collective-permute-start(bf16[128,1024]{1,0:T(8,128)(2,1)S(1)} %collective-permute-done.18.refs_1_), channel_id=1, source_target_pairs={{0,1},{1,0},{2,3},{3,2},{4,5},{5,4},{6,7},{7,6},{8,9},{9,8},{10,11... | collective-permute-start | bytes 786440 | tf_op jit(solution)/shard_map/ppermute | solution.py:17
  125.7 12.5 %collective-permute-start.23 = (bf16[128,1024]{1,0:T(8,128)(2,1)S(1)}, bf16[128,1024]{1,0:T(8,128)(2,1)}, u32[]{:S(2)}, u32[]{:S(2)}) collective-permute-start(bf16[128,1024]{1,0:T(8,128)(2,1)S(1)} %collective-permute-done.19.refs_2_), channel_id=1, source_target_pairs={{0,1},{1,0},{2,3},{3,2},{4,5},{5,4},{6,7},{7,6},{8,9},{9,8},{10,11... | collective-permute-start | bytes 786440 | tf_op jit(solution)/shard_map/ppermute | solution.py:17
  130.1 8.1 %collective-permute-start.24 = (bf16[128,1024]{1,0:T(8,128)(2,1)S(1)}, bf16[128,1024]{1,0:T(8,128)(2,1)}, u32[]{:S(2)}, u32[]{:S(2)}) collective-permute-start(bf16[128,1024]{1,0:T(8,128)(2,1)S(1)} %collective-permute-done.20.refs_3_), channel_id=1, source_target_pairs={{0,1},{1,0},{2,3},{3,2},{4,5},{5,4},{6,7},{7,6},{8,9},{9,8},{10,11... | collective-permute-start | bytes 786440 | tf_op jit(solution)/shard_map/ppermute | solution.py:17
  156.6 10.4 %collective-permute-start.25 = (bf16[512,1024]{1,0:T(8,128)(2,1)S(1)}, bf16[512,1024]{1,0:T(8,128)(2,1)S(1)}, u32[]{:S(2)}, u32[]{:S(2)}) collective-permute-start(bf16[512,1024]{1,0:T(8,128)(2,1)S(1)} %get-tuple-element.92), channel_id=1, source_target_pairs={{0,1},{1,0},{2,3},{3,2},{4,5},{5,4},{6,7},{7,6},{8,9},{9,8},{10,11... | collective-permute-start | bytes 3145736 | tf_op jit(solution)/shard_map/ppermute | solution.py:17
  168.5 84.1 %reduce-scatter.8.cloned.1.call-start = ((), (), s32[]{:S(2)}) async-start(), calls=%async_computation.11 | async-start | bytes 1638400 | tf_op jit(solution)/shard_map/reduce_scatter | solution.py:359
  169.9 8.4 %collective-permute-start.26 = (bf16[128,1024]{1,0:T(8,128)(2,1)S(1)}, bf16[128,1024]{1,0:T(8,128)(2,1)S(1)}, u32[]{:S(2)}, u32[]{:S(2)}) collective-permute-start(bf16[128,1024]{1,0:T(8,128)(2,1)S(1)} %get-tuple-element.140), channel_id=1, source_target_pairs={{0,2},{1,3},{2,0},{3,1},{4,6},{5,7},{6,4},{7,5},{8,10},{9,11},{10,... | collective-permute-start | bytes 786440 | tf_op jit(solution)/shard_map/ppermute | solution.py:17
  170.6 9.2 %collective-permute-start.27 = (bf16[128,1024]{1,0:T(8,128)(2,1)S(1)}, bf16[128,1024]{1,0:T(8,128)(2,1)S(1)}, u32[]{:S(2)}, u32[]{:S(2)}) collective-permute-start(bf16[128,1024]{1,0:T(8,128)(2,1)S(1)} %get-tuple-element.142), channel_id=1, source_target_pairs={{0,4},{1,5},{2,6},{3,7},{4,0},{5,1},{6,2},{7,3},{8,12},{9,13},{10,... | collective-permute-start | bytes 786440 | tf_op jit(solution)/shard_map/ppermute | solution.py:17
  170.9 14.1 %collective-permute-start.28 = (bf16[128,1024]{1,0:T(8,128)(2,1)S(1)}, bf16[128,1024]{1,0:T(8,128)(2,1)S(1)}, u32[]{:S(2)}, u32[]{:S(2)}) collective-permute-start(bf16[128,1024]{1,0:T(8,128)(2,1)S(1)} %get-tuple-element.141), channel_id=1, source_target_pairs={{0,6},{1,7},{2,4},{3,5},{4,2},{5,3},{6,0},{7,1},{8,14},{9,15},{10,... | collective-permute-start | bytes 786440 | tf_op jit(solution)/shard_map/ppermute | solution.py:17
  186.3 8.4 %collective-permute-start.29 = (bf16[128,1024]{1,0:T(8,128)(2,1)S(1)}, bf16[128,1024]{1,0:T(8,128)(2,1)}, u32[]{:S(2)}, u32[]{:S(2)}) collective-permute-start(bf16[128,1024]{1,0:T(8,128)(2,1)S(1)} %get-tuple-element.116), channel_id=1, source_target_pairs={{0,2},{1,3},{2,0},{3,1},{4,6},{5,7},{6,4},{7,5},{8,10},{9,11},{10,... | collective-permute-start | bytes 786440 | tf_op jit(solution)/shard_map/ppermute | solution.py:17
  186.9 9.3 %collective-permute-start.30 = (bf16[128,1024]{1,0:T(8,128)(2,1)S(1)}, bf16[128,1024]{1,0:T(8,128)(2,1)}, u32[]{:S(2)}, u32[]{:S(2)}) collective-permute-start(bf16[128,1024]{1,0:T(8,128)(2,1)S(1)} %get-tuple-element.116), channel_id=1, source_target_pairs={{0,4},{1,5},{2,6},{3,7},{4,0},{5,1},{6,2},{7,3},{8,12},{9,13},{10,... | collective-permute-start | bytes 786440 | tf_op jit(solution)/shard_map/ppermute | solution.py:17
  187.2 13.1 %collective-permute-start.31 = (bf16[128,1024]{1,0:T(8,128)(2,1)S(1)}, bf16[128,1024]{1,0:T(8,128)(2,1)}, u32[]{:S(2)}, u32[]{:S(2)}) collective-permute-start(bf16[128,1024]{1,0:T(8,128)(2,1)S(1)} %get-tuple-element.116), channel_id=1, source_target_pairs={{0,6},{1,7},{2,4},{3,5},{4,2},{5,3},{6,0},{7,1},{8,14},{9,15},{10,... | collective-permute-start | bytes 786440 | tf_op jit(solution)/shard_map/ppermute | solution.py:17
  189.8 12.1 %collective-permute-start.32 = (bf16[128,1024]{1,0:T(8,128)(2,1)S(1)}, bf16[128,1024]{1,0:T(8,128)(2,1)S(1)}, u32[]{:S(2)}, u32[]{:S(2)}) collective-permute-start(bf16[128,1024]{1,0:T(8,128)(2,1)S(1)} %get-tuple-element.116), channel_id=1, source_target_pairs={{0,1},{1,0},{2,3},{3,2},{4,5},{5,4},{6,7},{7,6},{8,9},{9,8},{10,11... | collective-permute-start | bytes 786440 | tf_op jit(solution)/shard_map/ppermute | solution.py:17
  194.8 7.1 %collective-permute-start.33 = (bf16[128,1024]{1,0:T(8,128)(2,1)}, bf16[128,1024]{1,0:T(8,128)(2,1)}, u32[]{:S(2)}, u32[]{:S(2)}) collective-permute-start(bf16[128,1024]{1,0:T(8,128)(2,1)} %collective-permute-done.29), channel_id=1, source_target_pairs={{0,1},{1,0},{2,3},{3,2},{4,5},{5,4},{6,7},{7,6},{8,9},{9,8},{10,11... | collective-permute-start | bytes 786440 | tf_op jit(solution)/shard_map/ppermute | solution.py:17
  214.2 14.3 %collective-permute-start.40 = (bf16[512,1024]{1,0:T(8,128)(2,1)}, bf16[512,1024]{1,0:T(8,128)(2,1)}, u32[]{:S(2)}, u32[]{:S(2)}) collective-permute-start(bf16[512,1024]{1,0:T(8,128)(2,1)} %convolution_convert_fusion.1), channel_id=1, source_target_pairs={{0,1},{1,0},{2,3},{3,2},{4,5},{5,4},{6,7},{7,6},{8,9},{9,8},{10,11... | collective-permute-start | bytes 3145736 | tf_op jit(solution)/shard_map/ppermute | solution.py:17
  220.3 14.0 %collective-permute-start.36 = (bf16[512,1024]{1,0:T(8,128)(2,1)}, bf16[512,1024]{1,0:T(8,128)(2,1)}, u32[]{:S(2)}, u32[]{:S(2)}) collective-permute-start(bf16[512,1024]{1,0:T(8,128)(2,1)} %split.7), channel_id=1, source_target_pairs={{0,1},{1,0},{2,3},{3,2},{4,5},{5,4},{6,7},{7,6},{8,9},{9,8},{10,11... | collective-permute-start | bytes 3145736 | tf_op jit(solution)/shard_map/ppermute | solution.py:17
  221.7 36.0 %all-to-all-start.3 = ((bf16[32,32,384]{2,1,0:T(8,128)(2,1)}), bf16[32,32,384]{2,1,0:T(8,128)(2,1)}, u32[]{:S(2)}, u32[]{:S(2)}) async-start(bf16[32,32,384]{2,1,0:T(8,128)(2,1)} %bitcast.276), calls=%async_computation.3 | async-start | bytes 1572864 | tf_op jit(solution)/shard_map/all_to_all | solution.py:393
  225.4 54.1 %reduce-scatter.4.cloned.1.call-start = ((), (), s32[]{:S(2)}) async-start(), calls=%async_computation.9 | async-start | bytes 1966080 | tf_op jit(solution)/shard_map/reduce_scatter | solution.py:404
  230.8 12.0 %collective-permute-start.41 = (bf16[128,1024]{1,0:T(8,128)(2,1)S(1)}, bf16[128,1024]{1,0:T(8,128)(2,1)S(1)}, u32[]{:S(2)}, u32[]{:S(2)}) collective-permute-start(bf16[128,1024]{1,0:T(8,128)(2,1)S(1)} %get-tuple-element.130), channel_id=1, source_target_pairs={{0,2},{1,3},{2,0},{3,1},{4,6},{5,7},{6,4},{7,5},{8,10},{9,11},{10,... | collective-permute-start | bytes 786440 | tf_op jit(solution)/shard_map/ppermute | solution.py:17
  232.5 12.2 %collective-permute-start.42 = (bf16[128,1024]{1,0:T(8,128)(2,1)S(1)}, bf16[128,1024]{1,0:T(8,128)(2,1)S(1)}, u32[]{:S(2)}, u32[]{:S(2)}) collective-permute-start(bf16[128,1024]{1,0:T(8,128)(2,1)S(1)} %get-tuple-element.132), channel_id=1, source_target_pairs={{0,4},{1,5},{2,6},{3,7},{4,0},{5,1},{6,2},{7,3},{8,12},{9,13},{10,... | collective-permute-start | bytes 786440 | tf_op jit(solution)/shard_map/ppermute | solution.py:17
  234.0 17.2 %collective-permute-start.43 = (bf16[128,1024]{1,0:T(8,128)(2,1)S(1)}, bf16[128,1024]{1,0:T(8,128)(2,1)S(1)}, u32[]{:S(2)}, u32[]{:S(2)}) collective-permute-start(bf16[128,1024]{1,0:T(8,128)(2,1)S(1)} %get-tuple-element.131), channel_id=1, source_target_pairs={{0,6},{1,7},{2,4},{3,5},{4,2},{5,3},{6,0},{7,1},{8,14},{9,15},{10,... | collective-permute-start | bytes 786440 | tf_op jit(solution)/shard_map/ppermute | solution.py:17
  236.1 26.0 %collective-permute-start.37 = (bf16[128,1024]{1,0:T(8,128)(2,1)S(1)}, bf16[128,1024]{1,0:T(8,128)(2,1)S(1)}, u32[]{:S(2)}, u32[]{:S(2)}) collective-permute-start(bf16[128,1024]{1,0:T(8,128)(2,1)S(1)} %get-tuple-element.137), channel_id=1, source_target_pairs={{0,2},{1,3},{2,0},{3,1},{4,6},{5,7},{6,4},{7,5},{8,10},{9,11},{10,... | collective-permute-start | bytes 786440 | tf_op jit(solution)/shard_map/ppermute | solution.py:17
  237.9 24.3 %collective-permute-start.38 = (bf16[128,1024]{1,0:T(8,128)(2,1)S(1)}, bf16[128,1024]{1,0:T(8,128)(2,1)S(1)}, u32[]{:S(2)}, u32[]{:S(2)}) collective-permute-start(bf16[128,1024]{1,0:T(8,128)(2,1)S(1)} %get-tuple-element.139), channel_id=1, source_target_pairs={{0,4},{1,5},{2,6},{3,7},{4,0},{5,1},{6,2},{7,3},{8,12},{9,13},{10,... | collective-permute-start | bytes 786440 | tf_op jit(solution)/shard_map/ppermute | solution.py:17
  242.8 19.4 %collective-permute-start.39 = (bf16[128,1024]{1,0:T(8,128)(2,1)S(1)}, bf16[128,1024]{1,0:T(8,128)(2,1)S(1)}, u32[]{:S(2)}, u32[]{:S(2)}) collective-permute-start(bf16[128,1024]{1,0:T(8,128)(2,1)S(1)} %get-tuple-element.138), channel_id=1, source_target_pairs={{0,6},{1,7},{2,4},{3,5},{4,2},{5,3},{6,0},{7,1},{8,14},{9,15},{10,... | collective-permute-start | bytes 786440 | tf_op jit(solution)/shard_map/ppermute | solution.py:17
  257.7 14.4 %all-to-all-start.4 = ((bf16[8,2,32,576]{3,2,1,0:T(8,128)(2,1)}), bf16[8,2,32,576]{3,2,1,0:T(8,128)(2,1)}, u32[]{:S(2)}, u32[]{:S(2)}) async-start(bf16[8,2,32,576]{3,2,1,0:T(8,128)(2,1)} %maximum_bitcast_fusion), calls=%async_computation.7 | async-start | bytes 1310720 | tf_op jit(solution)/shard_map/all_to_all | solution.py:403
  (85 other events, 316.9 us)
Sparse Core Ops, SparseCore 0:
  19.6 49.7 all-gather.5
  75.1 49.7 all-gather.3
  168.6 30.0 reduce-scatter.5
  200.9 30.0 reduce-scatter.7
  233.1 37.3 reduce-scatter.3

commit v2 on v1

--- a/solution.py
+++ b/solution.py
@@ -44,10 +44,9 @@
     return jnp.concatenate(blocks[:half]), jnp.concatenate(blocks[half:])
 
 
-def ffn_rows(steps, count, *refs):
+def ffn_first(steps, count, *refs):
     n2_blocks, seed_blocks = refs[:count], refs[count : 2 * count]
-    gate_w, up_w, down_w, n2, seed, hid, dgate, dup, mix, same, other = refs[2 * count :]
-    f32, bf = jnp.float32, jnp.bfloat16
+    gate_w, down_w, n2, seed, gate, d_hidden = refs[2 * count :]
     rows = n2_blocks[0].shape[0]
     for k in range(count):
 
@@ -57,15 +56,18 @@
             n2[at : at + rows, :] = n2_blocks[k][...]
             seed[at : at + rows, :] = seed_blocks[k][...]
 
-    x = n2[...]
-    gate = jnp.dot(x, gate_w[...], preferred_element_type=f32)
-    up = jnp.dot(x, up_w[...], preferred_element_type=f32)
+    gate[...] = dot(n2[...], gate_w[...])
+    d_hidden[...] = against(seed[...], down_w[...])
+
+
+def ffn_rows(n2, gate_in, d_hidden_in, gate_w, up_w, hid, dgate, dup, same, other):
+    bf = jnp.bfloat16
+    up = dot(n2[...], up_w[...])
+    gate = gate_in[...]
+    d_hidden = d_hidden_in[...]
     sig = 1.0 / (1.0 + jnp.exp(-gate))
     swish = gate * sig
-    h = (swish * up).astype(bf)
-    hid[...] = h
-    mix[...] = jnp.dot(h, down_w[...], preferred_element_type=f32).astype(bf)
-    d_hidden = against(seed[...], down_w[...])
+    hid[...] = (swish * up).astype(bf)
     dg = (d_hidden * up * sig * (1.0 + gate * (1.0 - sig))).astype(bf)
     du = (d_hidden * swish).astype(bf)
     dgate[...] = dg
@@ -92,30 +94,53 @@
     f32, bf = jnp.float32, jnp.bfloat16
     row = lambda width: pl.BlockSpec((tile, width), lambda i: (i, 0))
     whole = lambda w: pl.BlockSpec(w.shape, lambda i: (0, 0))
-    operands = (*n2_blocks, *seed_blocks, w_gate, w_up, w_down)
-    widths = [features, features, part, part, part, features]
-    return pl.pallas_call(
-        functools.partial(ffn_rows, steps, count),
+    shape = lambda width, kind: jax.ShapeDtypeStruct((rows, width), kind)
+    params = pltpu.CompilerParams(vmem_limit_bytes=48 * 2**20)
+    operands = (*n2_blocks, *seed_blocks, w_gate, w_down)
+    n2, seed, gate, d_hidden = pl.pallas_call(
+        functools.partial(ffn_first, steps, count),
         grid=(steps,),
         in_specs=[whole(w) for w in operands],
-        out_specs=[row(width) for width in widths]
-        + [
+        out_specs=[row(features), row(features), row(part), row(part)],
+        out_shape=[
+            shape(features, bf),
+            shape(features, bf),
+            shape(part, f32),
+            shape(part, f32),
+        ],
+        compiler_params=params,
+        cost_estimate=pl.CostEstimate(
+            flops=4 * rows * features * part,
+            bytes_accessed=4 * features * part + 8 * rows * features + 8 * rows * part,
+            transcendentals=0,
+        ),
+        name="ffn_first",
+    )(*operands)
+    hidden, d_gate, d_up, d_same, d_other = pl.pallas_call(
+        ffn_rows,
+        grid=(steps,),
+        in_specs=[row(features), row(part), row(part), whole(w_gate), whole(w_up)],
+        out_specs=[
+            row(part),
+            row(part),
+            row(part),
             pl.BlockSpec((tile, features), lambda i: (jnp.minimum(i, steps // 2 - 1), 0)),
             pl.BlockSpec((tile, features), lambda i: (jnp.maximum(i - steps // 2, 0), 0)),
         ],
-        out_shape=[jax.ShapeDtypeStruct((rows, width), bf) for width in widths]
+        out_shape=[shape(part, bf), shape(part, bf), shape(part, bf)]
         + [
             jax.ShapeDtypeStruct((rows // 2, features), f32),
             jax.ShapeDtypeStruct((rows // 2, features), bf),
         ],
-        compiler_params=pltpu.CompilerParams(vmem_limit_bytes=48 * 2**20),
+        compiler_params=params,
         cost_estimate=pl.CostEstimate(
-            flops=12 * rows * features * part,
-            bytes_accessed=6 * features * part + 14 * rows * features + 6 * rows * part,
+            flops=6 * rows * features * part,
+            bytes_accessed=4 * features * part + 5 * rows * features + 14 * rows * part,
             transcendentals=rows * part,
         ),
         name="ffn_rows",
-    )(*operands)
+    )(n2, gate, d_hidden, w_gate, w_up)
+    return n2, seed, hidden, d_gate, d_up, d_same, d_other
 
 
 def ffn_sums(n2, seed, hid, dgate, dup, g_gate, g_up, g_down, turned):
@@ -279,10 +304,10 @@
 
     gu_cut = jnp.stack([cut_ff(gate_weight), cut_ff(up_weight)], axis=1)
     gu_cut = lax.all_to_all(gu_cut, PLANE, split_axis=0, concat_axis=0, tiled=True)
-    gu_rows = gu_cut.transpose(1, 0, 2, 3).reshape(2, members * own, part_ff)
-    gu_all = lax.all_gather(gu_rows, "far", axis=0, tiled=False)
-    w_gate = gu_all[:, 0].reshape(features, part_ff)
-    w_up = gu_all[:, 1].reshape(features, part_ff)
+    w_gate = lax.all_gather(
+        gu_cut[:, 0].reshape(members * own, part_ff), "far", axis=0, tiled=True
+    )
+    w_up = lax.all_gather(gu_cut[:, 1].reshape(members * own, part_ff), "far", axis=0, tiled=True)
 
     seg_true = seg_all.reshape(n_near, n_ctx, seq_count, seq_rows).transpose(0, 2, 1, 3)
     me_near = lax.axis_index("near")
@@ -345,7 +370,7 @@
     normed2 = resid * inverse2
 
     n2_all = collect(normed2.astype(bf))
-    n2_all, seed_all, hidden, d_gate, d_up, part_mixed, d_same, d_other = ffn(
+    n2_all, seed_all, hidden, d_gate, d_up, d_same, d_other = ffn(
         n2_all, seed_all, w_gate, w_up, w_down
     )
     sum_gate, sum_up, sum_down = weight_sums(n2_all, seed_all, hidden, d_gate, d_up)
@@ -363,8 +388,9 @@
 
     d_branch = collect(d_resid.astype(bf))
     d_branch = halves(d_branch)
-    d_branch, part_mixed = lax.optimization_barrier((d_branch, part_mixed))
-    mixed = (resid + reduce_rows(*[m.astype(f32) for m in jnp.split(part_mixed, 2)])).astype(bf)
+    d_branch, hidden = lax.optimization_barrier((d_branch, hidden))
+    mixed = resid + reduce_rows(*[dot(h, w_down) for h in jnp.split(hidden, 2)])
+    mixed = mixed.astype(bf)
     d_gated = [against(d, w_out) for d in d_branch]
     d_short = to_true(*[(d * c).astype(bf) for d, c in zip(d_gated, part_c)]).astype(f32)
     sum_taps = jnp.stack(

time: 291 us -> 289 us (level)
  local copies, waits for them, and re-layouts: 48.6 us -> 33.5 us
  matrix products: 13.9 us -> 22.7 us
    all_gather x1 -> x2, waiting for transfers between devices: 0.01 us -> 9.46 us  [the longest x1 9.44 us: on_device(): lax.all_gather(gu_cut[:, 1].reshape(members * own, part_ff), 'far', axis=...]
    slice x3 -> x1, local copies, waits for them, and re-layouts: 8.07 us -> 0.89 us  [on_device(): gu_cut[:, 1].reshape(members * own, part_ff)]
    dot_general x4 -> x6, matrix products: 3.67 us -> 9.14 us  [dot(): return jnp.dot(a, b, preferred_element_type=jnp.float32)]
    ppermute x44, waiting for transfers between devices: 81.2 us -> 76 us  [mate(): return lax.ppermute(value, PLANE, [(k, k ^ flip) for k in range(count)])]
    another operation x3, local copies, waits for them, and re-layouts: 3.35 us -> 0.25 us  [on_device(): jnp.stack([jnp.sum(d_short * earlier, axis=(0, 1)), jnp.sum(d_short * pre...]
    all_to_all x1, waiting for transfers between devices: 8.8 us -> 5.73 us  [on_device(): lax.all_to_all(gu_cut, PLANE, split_axis=0, concat_axis=0, tiled=True)]
    pallas_call x1 -> x2, Pallas kernels: 18.4 us -> 17 us  [the longest x1 9.97 us: ffn(): pl.pallas_call(ffn_rows, grid=(steps,), in_specs=[row(features), row(part...]
    unnamed x163 -> x167, local copies, waits for them, and re-layouts: 9.91 us -> 9.48 us
  transfers between devices with their start and end apart: 54 -> 55, of which waited for: 28 -> 28; matrix products, arithmetic and copies ran while one was open for 27% -> 25% of each run, Pallas kernels for 3% -> 6%
where the time goes in v2:
time: 289 us; the launch traced here: 288 us
  waiting for transfers between devices  100 us (35%)
  starting transfers between devices  56.7 us (20%)
  local copies, waits for them, and re-layouts  33.5 us (12%)
  other arithmetic  32.9 us (11%)
  Pallas kernels  26 us (9%)
  matrix products  22.7 us (8%)
  between operations  15.7 us (5%)
    ppermute x44, waiting for transfers between devices, mate(): return lax.ppermute(value, PLANE, [(k, k ^ flip) for k in range(count)])  76 us
    ppermute x44, starting transfers between devices, mate(): return lax.ppermute(value, PLANE, [(k, k ^ flip) for k in range(count)])  31.9 us
    pallas_call x1, Pallas kernels, ffn(): pl.pallas_call(ffn_rows, grid=(steps,), in_specs=[row(features), row(part...  9.97 us
    unnamed x167, local copies, waits for them, and re-layouts  9.48 us
    all_gather x1, waiting for transfers between devices, on_device(): lax.all_gather(gu_cut[:, 1].reshape(members * own, part_ff), 'far', axis=...  9.44 us
    dot_general x6, matrix products, dot(): return jnp.dot(a, b, preferred_element_type=jnp.float32)  9.14 us
    pallas_call x1, Pallas kernels, weight_sums(): pl.pallas_call(ffn_sums, grid=(4,), in_specs=[column(rows), column(rows),...  8.92 us
    all_to_all x1, starting transfers between devices, on_device(): lax.all_to_all(small, everyone, split_axis=0, concat_axis=0, tiled=True)  7.3 us
  transfers between devices with their start and end apart: 55, of which 28 were waited for; matrix products, arithmetic and copies ran while one was open for 25% of the time, Pallas kernels for 6%

profile of v2, /device:TPU:0, one launch (start us, length us, event | category | flops | bytes accessed | tf_op | source)
XLA Modules:
  0.0 287.9 jit_solution(14705171799280431926)
XLA Ops:
  9.3 7.3 %all-to-all-start = ((bf16[32,16,128]{2,1,0:T(8,128)(2,1)}), bf16[32,16,128]{2,1,0:T(8,128)(2,1)S(1)}, u32[]{:S(2)}, u32[]{:S(2)}) async-start(bf16[32,16,128]{2,1,0:T(8,128)(2,1)} %broadcast_in_dim.6), calls=%async_computation | async-start | bytes 262144 | tf_op jit(solution)/shard_map/all_to_all | solution.py:281
  16.7 1.8 fusion.25
  24.8 3.5 %all-to-all-start.2 = ((bf16[8,2,32,576]{3,2,1,0:T(8,128)(2,1)}), bf16[8,2,32,576]{3,2,1,0:T(8,128)(2,1)S(1)}, u32[]{:S(2)}, u32[]{:S(2)}) async-start(bf16[8,2,32,576]{3,2,1,0:T(8,128)(2,1)} %pad_maximum_fusion.4), calls=%async_computation.2 | async-start | bytes 1310720 | tf_op jit(solution)/shard_map/all_to_all | solution.py:306
  28.4 1.9 collective-permute-start
  33.3 5.7 %all-to-all-done.2 = bf16[8,2,32,576]{3,2,1,0:T(8,128)(2,1)S(1)} async-done(((bf16[8,2,32,576]{3,2,1,0:T(8,128)(2,1)}), bf16[8,2,32,576]{3,2,1,0:T(8,128)(2,1)S(1)}, u32[]{:S(2)}, u32[]{:S(2)}) %all-to-all-start.2) | async-done | bytes 589856 | tf_op jit(solution)/shard_map/all_to_all | solution.py:306
  40.0 4.4 %all-to-all-start.1 = ((bf16[32,32,384]{2,1,0:T(8,128)(2,1)}), bf16[32,32,384]{2,1,0:T(8,128)(2,1)S(1)}, u32[]{:S(2)}, u32[]{:S(2)}) async-start(bf16[32,32,384]{2,1,0:T(8,128)(2,1)} %bitcast.7), calls=%async_computation.1 | async-start | bytes 1572864 | tf_op jit(solution)/shard_map/all_to_all | solution.py:290
  45.5 6.3 %collective-permute-done.2 = bf16[128,1024]{1,0:T(8,128)(2,1)} collective-permute-done((bf16[128,1024]{1,0:T(8,128)(2,1)S(1)}, bf16[128,1024]{1,0:T(8,128)(2,1)}, u32[]{:S(2)}, u32[]{:S(2)}) %collective-permute-start.2) | collective-permute-done | bytes 262176 | tf_op jit(solution)/shard_map/ppermute | solution.py:17
  55.1 2.6 collective-permute-start.9
  58.8 1.8 fusion.1
  60.5 4.1 %collective-permute-done.7.refs_9_ = bf16[128,1024]{1,0:T(8,128)(2,1)S(1)} collective-permute-done((bf16[128,1024]{1,0:T(8,128)(2,1)S(1)}, bf16[128,1024]{1,0:T(8,128)(2,1)S(1)}, u32[]{:S(2)}, u32[]{:S(2)}) %collective-permute-start.7) | collective-permute-done | bytes 262176 | tf_op jit(solution)/shard_map/ppermute | solution.py:17
  65.6 7.3 %collective-permute-done.9.refs_11_ = bf16[128,1024]{1,0:T(8,128)(2,1)S(1)} collective-permute-done((bf16[128,1024]{1,0:T(8,128)(2,1)S(1)}, bf16[128,1024]{1,0:T(8,128)(2,1)S(1)}, u32[]{:S(2)}, u32[]{:S(2)}) %collective-permute-start.9) | collective-permute-done | bytes 262176 | tf_op jit(solution)/shard_map/ppermute | solution.py:17
  75.2 2.1 fusion.31
  87.7 1.8 fusion.47
  93.2 4.8 %collective-permute-done.15 = bf16[128,1024]{1,0:T(8,128)(2,1)S(1)} collective-permute-done((bf16[128,1024]{1,0:T(8,128)(2,1)S(1)}, bf16[128,1024]{1,0:T(8,128)(2,1)S(1)}, u32[]{:S(2)}, u32[]{:S(2)}) %collective-permute-start.15) | collective-permute-done | bytes 262176 | tf_op jit(solution)/shard_map/ppermute | solution.py:17
  99.6 5.2 %collective-permute-done.17 = bf16[128,1024]{1,0:T(8,128)(2,1)S(1)} collective-permute-done((bf16[128,1024]{1,0:T(8,128)(2,1)S(1)}, bf16[128,1024]{1,0:T(8,128)(2,1)S(1)}, u32[]{:S(2)}, u32[]{:S(2)}) %collective-permute-start.17) | collective-permute-done | bytes 262176 | tf_op jit(solution)/shard_map/ppermute | solution.py:17
  108.7 5.0 %collective-permute-done.18.refs_1_ = bf16[128,1024]{1,0:T(8,128)(2,1)} collective-permute-done((bf16[128,1024]{1,0:T(8,128)(2,1)S(1)}, bf16[128,1024]{1,0:T(8,128)(2,1)}, u32[]{:S(2)}, u32[]{:S(2)}) %collective-permute-start.18) | collective-permute-done | bytes 262176 | tf_op jit(solution)/shard_map/ppermute | solution.py:17
  113.7 1.7 collective-permute-done.19.refs_2_
  115.4 4.0 %collective-permute-done.20.refs_3_ = bf16[128,1024]{1,0:T(8,128)(2,1)} collective-permute-done((bf16[128,1024]{1,0:T(8,128)(2,1)S(1)}, bf16[128,1024]{1,0:T(8,128)(2,1)}, u32[]{:S(2)}, u32[]{:S(2)}) %collective-permute-start.20) | collective-permute-done | bytes 262176 | tf_op jit(solution)/shard_map/ppermute | solution.py:17
  119.6 1.7 collective-permute-done.24.refs_7_
  122.3 7.1 %ffn_first.1 = (bf16[1024,1024]{1,0:T(8,128)(2,1)}, bf16[1024,1024]{1,0:T(8,128)(2,1)}, f32[1024,576]{1,0:T(8,128)}, f32[1024,576]{1,0:T(8,128)}) custom-call(bf16[128,1024]{1,0:T(8,128)(2,1)S(1)} %multiply_convert_fusion.refs_0_, bf16[128,1024]{1,0:T(8,128)(2,1)} %collective-permute-done.18.refs_1_, bf16[128,1024]{1,0:T(8,128)(2,1)} %collective-permute-done.19.refs_2_, ...), custom_call_target="tpu_custom_call" | custom-call | flops 2415919104 | bytes 15466496 | tf_op jit(solution)/shard_map/ffn_first/pallas_call | solution.py:100
  129.4 9.4 %all-gather.7.cloned.1.call-done.up_w = bf16[1024,576]{1,0:T(8,128)(2,1)} async-done(((bf16[256,576]{1,0:T(8,128)(2,1)}), bf16[1024,576]{1,0:T(8,128)(2,1)}) %all-gather.7.cloned.1.call-update) | async-done | bytes 1179664 | tf_op jit(solution)/shard_map/all_gather | solution.py:310
  138.8 10.0 %ffn_rows.1 = (bf16[1024,576]{1,0:T(8,128)(2,1)S(1)}, bf16[1024,576]{1,0:T(8,128)(2,1)S(1)}, bf16[1024,576]{1,0:T(8,128)(2,1)S(1)}, f32[512,1024]{1,0:T(8,128)}, bf16[512,1024]{1,0:T(8,128)(2,1)S(1)}) custom-call(bf16[1024,1024]{1,0:T(8,128)(2,1)} %get-tuple-element.92.n2, f32[1024,576]{1,0:T(8,128)} %get-tuple-element.93.gate_in, ...), custom_call_target="tpu_custom_call" | custom-call | flops 3623878656 | bytes 15859712 | tf_op jit(solution)/shard_map/ffn_rows/pallas_call | solution.py:119
  150.9 8.9 %ffn_sums.1 = (bf16[1024,576]{1,0:T(8,128)(2,1)}, bf16[1024,576]{1,0:T(8,128)(2,1)}, bf16[576,1024]{1,0:T(8,128)(2,1)S(1)}) custom-call(bf16[1024,1024]{1,0:T(8,128)(2,1)} %get-tuple-element.92.n2, bf16[1024,1024]{1,0:T(8,128)(2,1)} %get-tuple-element.97.seed, bf16[1024,576]{1,0:T(8,128)(2,1)S(1)} %get-tuple-element.105.hid, bf16[1024,576]{1,0:T(8,128)(2,1)} %copy-done.6, ...), custom_call_target="tpu_custom_call" | custom-call | flops 3623878656 | bytes 11272192 | tf_op jit(solution)/shard_map/ffn_sums/pallas_call | solution.py:164
  167.2 4.9 %collective-permute-done.26 = bf16[128,1024]{1,0:T(8,128)(2,1)S(1)} collective-permute-done((bf16[128,1024]{1,0:T(8,128)(2,1)S(1)}, bf16[128,1024]{1,0:T(8,128)(2,1)S(1)}, u32[]{:S(2)}, u32[]{:S(2)}) %collective-permute-start.26) | collective-permute-done | bytes 262176 | tf_op jit(solution)/shard_map/ppermute | solution.py:17
  172.1 2.3 collective-permute-done.27
  174.4 4.5 %collective-permute-done.28 = bf16[128,1024]{1,0:T(8,128)(2,1)S(1)} collective-permute-done((bf16[128,1024]{1,0:T(8,128)(2,1)S(1)}, bf16[128,1024]{1,0:T(8,128)(2,1)S(1)}, u32[]{:S(2)}, u32[]{:S(2)}) %collective-permute-start.28) | collective-permute-done | bytes 262176 | tf_op jit(solution)/shard_map/ppermute | solution.py:17
  185.0 4.9 %collective-permute-done.29 = bf16[128,1024]{1,0:T(8,128)(2,1)S(1)} collective-permute-done((bf16[128,1024]{1,0:T(8,128)(2,1)}, bf16[128,1024]{1,0:T(8,128)(2,1)S(1)}, u32[]{:S(2)}, u32[]{:S(2)}) %collective-permute-start.29) | collective-permute-done | bytes 262176 | tf_op jit(solution)/shard_map/ppermute | solution.py:17
  189.8 2.5 collective-permute-done.30
  192.3 3.3 %collective-permute-done.31 = bf16[128,1024]{1,0:T(8,128)(2,1)} collective-permute-done((bf16[128,1024]{1,0:T(8,128)(2,1)}, bf16[128,1024]{1,0:T(8,128)(2,1)}, u32[]{:S(2)}, u32[]{:S(2)}) %collective-permute-start.31) | collective-permute-done | bytes 262176 | tf_op jit(solution)/shard_map/ppermute | solution.py:17
  209.6 1.9 fusion.29
  211.6 1.8 add_convert_fusion
  213.3 1.7 convolution_convert_fusion.1
  215.6 2.0 convolution_convert_fusion.2
  218.8 3.8 %all-to-all-start.3 = ((bf16[32,32,384]{2,1,0:T(8,128)(2,1)}), bf16[32,32,384]{2,1,0:T(8,128)(2,1)}, u32[]{:S(2)}, u32[]{:S(2)}) async-start(bf16[32,32,384]{2,1,0:T(8,128)(2,1)} %bitcast.276), calls=%async_computation.3 | async-start | bytes 1572864 | tf_op jit(solution)/shard_map/all_to_all | solution.py:419
  222.6 1.7 fusion.8
  226.8 2.1 fusion.63
  229.0 1.8 collective-permute-start.41
  232.5 2.4 fusion.62
  235.1 1.7 collective-permute-start.37
  238.3 1.7 collective-permute-done.41
  240.0 2.3 collective-permute-start.39
  242.3 5.9 %collective-permute-done.43 = bf16[128,1024]{1,0:T(8,128)(2,1)S(1)} collective-permute-done((bf16[128,1024]{1,0:T(8,128)(2,1)S(1)}, bf16[128,1024]{1,0:T(8,128)(2,1)S(1)}, u32[]{:S(2)}, u32[]{:S(2)}) %collective-permute-start.43) | collective-permute-done | bytes 262176 | tf_op jit(solution)/shard_map/ppermute | solution.py:17
  249.6 2.0 maximum_bitcast_fusion
  251.6 3.4 %all-to-all-done.3 = bf16[32,32,384]{2,1,0:T(8,128)(2,1)} async-done(((bf16[32,32,384]{2,1,0:T(8,128)(2,1)}), bf16[32,32,384]{2,1,0:T(8,128)(2,1)}, u32[]{:S(2)}, u32[]{:S(2)}) %all-to-all-start.3) | async-done | bytes 786464 | tf_op jit(solution)/shard_map/all_to_all | solution.py:419
  255.0 5.1 %all-to-all-start.4 = ((bf16[8,2,32,576]{3,2,1,0:T(8,128)(2,1)}), bf16[8,2,32,576]{3,2,1,0:T(8,128)(2,1)}, u32[]{:S(2)}, u32[]{:S(2)}) async-start(bf16[8,2,32,576]{3,2,1,0:T(8,128)(2,1)} %maximum_bitcast_fusion), calls=%async_computation.7 | async-start | bytes 1310720 | tf_op jit(solution)/shard_map/all_to_all | solution.py:429
  265.4 5.0 %all-to-all-done.4 = bf16[8,2,32,576]{3,2,1,0:T(8,128)(2,1)} async-done(((bf16[8,2,32,576]{3,2,1,0:T(8,128)(2,1)}), bf16[8,2,32,576]{3,2,1,0:T(8,128)(2,1)}, u32[]{:S(2)}, u32[]{:S(2)}) %all-to-all-start.4) | async-done | bytes 589856 | tf_op jit(solution)/shard_map/all_to_all | solution.py:429
  270.4 2.8 reshape.698
  275.9 1.8 broadcast_multiply_fusion
  (381 shorter events, 90.5 us)
Async XLA Ops:
  9.3 15.5 %all-to-all-start = ((bf16[32,16,128]{2,1,0:T(8,128)(2,1)}), bf16[32,16,128]{2,1,0:T(8,128)(2,1)S(1)}, u32[]{:S(2)}, u32[]{:S(2)}) async-start(bf16[32,16,128]{2,1,0:T(8,128)(2,1)} %broadcast_in_dim.6), calls=%async_computation | async-start | bytes 262144 | tf_op jit(solution)/shard_map/all_to_all | solution.py:281
  16.6 62.7 %all-gather.9.cloned.1.call-start = ((), (), s32[]{:S(2)}) async-start(), calls=%async_computation.13 | async-start | bytes 1966080 | tf_op jit(solution)/shard_map/all_gather | solution.py:294
  24.8 14.2 %all-to-all-start.2 = ((bf16[8,2,32,576]{3,2,1,0:T(8,128)(2,1)}), bf16[8,2,32,576]{3,2,1,0:T(8,128)(2,1)S(1)}, u32[]{:S(2)}, u32[]{:S(2)}) async-start(bf16[8,2,32,576]{3,2,1,0:T(8,128)(2,1)} %pad_maximum_fusion.4), calls=%async_computation.2 | async-start | bytes 1310720 | tf_op jit(solution)/shard_map/all_to_all | solution.py:306
  28.4 16.5 %collective-permute-start = (bf16[128,1024]{1,0:T(8,128)(2,1)S(1)}, bf16[128,1024]{1,0:T(8,128)(2,1)S(1)}, u32[]{:S(2)}, u32[]{:S(2)}) collective-permute-start(bf16[128,1024]{1,0:T(8,128)(2,1)S(1)} %bitcast.226), channel_id=1, source_target_pairs={{0,2},{1,3},{2,0},{3,1},{4,6},{5,7},{6,4},{7,5},{8,10},{9,11},{10,... | collective-permute-start | bytes 786440 | tf_op jit(solution)/shard_map/ppermute | solution.py:17
  30.3 14.9 %collective-permute-start.1 = (bf16[128,1024]{1,0:T(8,128)(2,1)S(1)}, bf16[128,1024]{1,0:T(8,128)(2,1)}, u32[]{:S(2)}, u32[]{:S(2)}) collective-permute-start(bf16[128,1024]{1,0:T(8,128)(2,1)S(1)} %bitcast.227), channel_id=1, source_target_pairs={{0,4},{1,5},{2,6},{3,7},{4,0},{5,1},{6,2},{7,3},{8,12},{9,13},{10,... | collective-permute-start | bytes 786440 | tf_op jit(solution)/shard_map/ppermute | solution.py:17
  31.8 19.9 %collective-permute-start.2 = (bf16[128,1024]{1,0:T(8,128)(2,1)S(1)}, bf16[128,1024]{1,0:T(8,128)(2,1)}, u32[]{:S(2)}, u32[]{:S(2)}) collective-permute-start(bf16[128,1024]{1,0:T(8,128)(2,1)S(1)} %bitcast.228), channel_id=1, source_target_pairs={{0,6},{1,7},{2,4},{3,5},{4,2},{5,3},{6,0},{7,1},{8,14},{9,15},{10,... | collective-permute-start | bytes 786440 | tf_op jit(solution)/shard_map/ppermute | solution.py:17
  40.0 35.1 %all-to-all-start.1 = ((bf16[32,32,384]{2,1,0:T(8,128)(2,1)}), bf16[32,32,384]{2,1,0:T(8,128)(2,1)S(1)}, u32[]{:S(2)}, u32[]{:S(2)}) async-start(bf16[32,32,384]{2,1,0:T(8,128)(2,1)} %bitcast.7), calls=%async_computation.1 | async-start | bytes 1572864 | tf_op jit(solution)/shard_map/all_to_all | solution.py:290
  44.4 75.2 %all-gather.5.cloned.1.call-start = ((), (), s32[]{:S(2)}) async-start(), calls=%async_computation.8 | async-start | bytes 1638400 | tf_op jit(solution)/shard_map/all_gather | solution.py:307
  44.5 7.6 %collective-permute-start.3 = (bf16[128,1024]{1,0:T(8,128)(2,1)S(1)}, bf16[128,1024]{1,0:T(8,128)(2,1)S(1)}, u32[]{:S(2)}, u32[]{:S(2)}) collective-permute-start(bf16[128,1024]{1,0:T(8,128)(2,1)S(1)} %bitcast.229), channel_id=1, source_target_pairs={{0,1},{1,0},{2,3},{3,2},{4,5},{5,4},{6,7},{7,6},{8,9},{9,8},{10,11... | collective-permute-start | bytes 786440 | tf_op jit(solution)/shard_map/ppermute | solution.py:17
  44.9 7.2 %collective-permute-start.4 = (bf16[128,1024]{1,0:T(8,128)(2,1)S(1)}, bf16[128,1024]{1,0:T(8,128)(2,1)S(1)}, u32[]{:S(2)}, u32[]{:S(2)}) collective-permute-start(bf16[128,1024]{1,0:T(8,128)(2,1)S(1)} %collective-permute-done), channel_id=1, source_target_pairs={{0,1},{1,0},{2,3},{3,2},{4,5},{5,4},{6,7},{7,6},{8,9},{9,8},{10,11... | collective-permute-start | bytes 786440 | tf_op jit(solution)/shard_map/ppermute | solution.py:17
  45.2 6.9 %collective-permute-start.5 = (bf16[128,1024]{1,0:T(8,128)(2,1)}, bf16[128,1024]{1,0:T(8,128)(2,1)S(1)}, u32[]{:S(2)}, u32[]{:S(2)}) collective-permute-start(bf16[128,1024]{1,0:T(8,128)(2,1)} %collective-permute-done.1), channel_id=1, source_target_pairs={{0,1},{1,0},{2,3},{3,2},{4,5},{5,4},{6,7},{7,6},{8,9},{9,8},{10,11... | collective-permute-start | bytes 786440 | tf_op jit(solution)/shard_map/ppermute | solution.py:17
  54.2 10.4 %collective-permute-start.7 = (bf16[128,1024]{1,0:T(8,128)(2,1)S(1)}, bf16[128,1024]{1,0:T(8,128)(2,1)S(1)}, u32[]{:S(2)}, u32[]{:S(2)}) collective-permute-start(bf16[128,1024]{1,0:T(8,128)(2,1)S(1)} %bitcast.204), channel_id=1, source_target_pairs={{0,2},{1,3},{2,0},{3,1},{4,6},{5,7},{6,4},{7,5},{8,10},{9,11},{10,... | collective-permute-start | bytes 786440 | tf_op jit(solution)/shard_map/ppermute | solution.py:17
  54.5 11.0 %collective-permute-start.8 = (bf16[128,1024]{1,0:T(8,128)(2,1)S(1)}, bf16[128,1024]{1,0:T(8,128)(2,1)S(1)}, u32[]{:S(2)}, u32[]{:S(2)}) collective-permute-start(bf16[128,1024]{1,0:T(8,128)(2,1)S(1)} %bitcast.205), channel_id=1, source_target_pairs={{0,4},{1,5},{2,6},{3,7},{4,0},{5,1},{6,2},{7,3},{8,12},{9,13},{10,... | collective-permute-start | bytes 786440 | tf_op jit(solution)/shard_map/ppermute | solution.py:17
  55.1 17.8 %collective-permute-start.9 = (bf16[128,1024]{1,0:T(8,128)(2,1)S(1)}, bf16[128,1024]{1,0:T(8,128)(2,1)S(1)}, u32[]{:S(2)}, u32[]{:S(2)}) collective-permute-start(bf16[128,1024]{1,0:T(8,128)(2,1)S(1)} %bitcast.206), channel_id=1, source_target_pairs={{0,6},{1,7},{2,4},{3,5},{4,2},{5,3},{6,0},{7,1},{8,14},{9,15},{10,... | collective-permute-start | bytes 786440 | tf_op jit(solution)/shard_map/ppermute | solution.py:17
  58.6 80.2 %all-gather.7.cloned.1.call-start = ((), (), s32[]{:S(2)}) async-start(), calls=%async_computation.9 | async-start | bytes 1638400 | tf_op jit(solution)/shard_map/all_gather | solution.py:310
  58.7 14.8 %collective-permute-start.10 = (bf16[128,1024]{1,0:T(8,128)(2,1)S(1)}, bf16[128,1024]{1,0:T(8,128)(2,1)S(1)}, u32[]{:S(2)}, u32[]{:S(2)}) collective-permute-start(bf16[128,1024]{1,0:T(8,128)(2,1)S(1)} %bitcast.207), channel_id=1, source_target_pairs={{0,1},{1,0},{2,3},{3,2},{4,5},{5,4},{6,7},{7,6},{8,9},{9,8},{10,11... | collective-permute-start | bytes 786440 | tf_op jit(solution)/shard_map/ppermute | solution.py:17
  64.6 8.9 %collective-permute-start.11 = (bf16[128,1024]{1,0:T(8,128)(2,1)S(1)}, bf16[128,1024]{1,0:T(8,128)(2,1)S(1)}, u32[]{:S(2)}, u32[]{:S(2)}) collective-permute-start(bf16[128,1024]{1,0:T(8,128)(2,1)S(1)} %collective-permute-done.7.refs_9_), channel_id=1, source_target_pairs={{0,1},{1,0},{2,3},{3,2},{4,5},{5,4},{6,7},{7,6},{8,9},{9,8},{10,11... | collective-permute-start | bytes 786440 | tf_op jit(solution)/shard_map/ppermute | solution.py:17
  65.6 7.9 %collective-permute-start.12 = (bf16[128,1024]{1,0:T(8,128)(2,1)S(1)}, bf16[128,1024]{1,0:T(8,128)(2,1)S(1)}, u32[]{:S(2)}, u32[]{:S(2)}) collective-permute-start(bf16[128,1024]{1,0:T(8,128)(2,1)S(1)} %collective-permute-done.8.refs_10_), channel_id=1, source_target_pairs={{0,1},{1,0},{2,3},{3,2},{4,5},{5,4},{6,7},{7,6},{8,9},{9,8},{10,11... | collective-permute-start | bytes 786440 | tf_op jit(solution)/shard_map/ppermute | solution.py:17
  84.9 164.7 %reduce-scatter.6.cloned.1.call-start = ((), (), s32[]{:S(2)}) async-start(), calls=%async_computation.11 | async-start | bytes 1638400 | tf_op jit(solution)/shard_map/reduce_scatter | solution.py:383
  89.6 8.4 %collective-permute-start.15 = (bf16[128,1024]{1,0:T(8,128)(2,1)S(1)}, bf16[128,1024]{1,0:T(8,128)(2,1)S(1)}, u32[]{:S(2)}, u32[]{:S(2)}) collective-permute-start(bf16[128,1024]{1,0:T(8,128)(2,1)S(1)} %get-tuple-element.141), channel_id=1, source_target_pairs={{0,2},{1,3},{2,0},{3,1},{4,6},{5,7},{6,4},{7,5},{8,10},{9,11},{10,... | collective-permute-start | bytes 786440 | tf_op jit(solution)/shard_map/ppermute | solution.py:17
  90.4 9.2 %collective-permute-start.16 = (bf16[128,1024]{1,0:T(8,128)(2,1)S(1)}, bf16[128,1024]{1,0:T(8,128)(2,1)S(1)}, u32[]{:S(2)}, u32[]{:S(2)}) collective-permute-start(bf16[128,1024]{1,0:T(8,128)(2,1)S(1)} %get-tuple-element.143), channel_id=1, source_target_pairs={{0,4},{1,5},{2,6},{3,7},{4,0},{5,1},{6,2},{7,3},{8,12},{9,13},{10,... | collective-permute-start | bytes 786440 | tf_op jit(solution)/shard_map/ppermute | solution.py:17
  91.9 12.9 %collective-permute-start.17 = (bf16[128,1024]{1,0:T(8,128)(2,1)S(1)}, bf16[128,1024]{1,0:T(8,128)(2,1)S(1)}, u32[]{:S(2)}, u32[]{:S(2)}) collective-permute-start(bf16[128,1024]{1,0:T(8,128)(2,1)S(1)} %get-tuple-element.142), channel_id=1, source_target_pairs={{0,6},{1,7},{2,4},{3,5},{4,2},{5,3},{6,0},{7,1},{8,14},{9,15},{10,... | collective-permute-start | bytes 786440 | tf_op jit(solution)/shard_map/ppermute | solution.py:17
  105.2 8.5 %collective-permute-start.18 = (bf16[128,1024]{1,0:T(8,128)(2,1)S(1)}, bf16[128,1024]{1,0:T(8,128)(2,1)}, u32[]{:S(2)}, u32[]{:S(2)}) collective-permute-start(bf16[128,1024]{1,0:T(8,128)(2,1)S(1)} %multiply_convert_fusion.refs_0_), channel_id=1, source_target_pairs={{0,2},{1,3},{2,0},{3,1},{4,6},{5,7},{6,4},{7,5},{8,10},{9,11},{10,... | collective-permute-start | bytes 786440 | tf_op jit(solution)/shard_map/ppermute | solution.py:17
  106.0 9.3 %collective-permute-start.19 = (bf16[128,1024]{1,0:T(8,128)(2,1)S(1)}, bf16[128,1024]{1,0:T(8,128)(2,1)}, u32[]{:S(2)}, u32[]{:S(2)}) collective-permute-start(bf16[128,1024]{1,0:T(8,128)(2,1)S(1)} %multiply_convert_fusion.refs_0_), channel_id=1, source_target_pairs={{0,4},{1,5},{2,6},{3,7},{4,0},{5,1},{6,2},{7,3},{8,12},{9,13},{10,... | collective-permute-start | bytes 786440 | tf_op jit(solution)/shard_map/ppermute | solution.py:17
  107.6 11.9 %collective-permute-start.20 = (bf16[128,1024]{1,0:T(8,128)(2,1)S(1)}, bf16[128,1024]{1,0:T(8,128)(2,1)}, u32[]{:S(2)}, u32[]{:S(2)}) collective-permute-start(bf16[128,1024]{1,0:T(8,128)(2,1)S(1)} %multiply_convert_fusion.refs_0_), channel_id=1, source_target_pairs={{0,6},{1,7},{2,4},{3,5},{4,2},{5,3},{6,0},{7,1},{8,14},{9,15},{10,... | collective-permute-start | bytes 786440 | tf_op jit(solution)/shard_map/ppermute | solution.py:17
  108.7 10.8 %collective-permute-start.21 = (bf16[128,1024]{1,0:T(8,128)(2,1)S(1)}, bf16[128,1024]{1,0:T(8,128)(2,1)}, u32[]{:S(2)}, u32[]{:S(2)}) collective-permute-start(bf16[128,1024]{1,0:T(8,128)(2,1)S(1)} %multiply_convert_fusion.refs_0_), channel_id=1, source_target_pairs={{0,1},{1,0},{2,3},{3,2},{4,5},{5,4},{6,7},{7,6},{8,9},{9,8},{10,11... | collective-permute-start | bytes 786440 | tf_op jit(solution)/shard_map/ppermute | solution.py:17
  113.7 5.9 %collective-permute-start.22 = (bf16[128,1024]{1,0:T(8,128)(2,1)}, bf16[128,1024]{1,0:T(8,128)(2,1)}, u32[]{:S(2)}, u32[]{:S(2)}) collective-permute-start(bf16[128,1024]{1,0:T(8,128)(2,1)} %collective-permute-done.18.refs_1_), channel_id=1, source_target_pairs={{0,1},{1,0},{2,3},{3,2},{4,5},{5,4},{6,7},{7,6},{8,9},{9,8},{10,11... | collective-permute-start | bytes 786440 | tf_op jit(solution)/shard_map/ppermute | solution.py:17
  150.9 8.9 %collective-permute-start.25 = (bf16[512,1024]{1,0:T(8,128)(2,1)S(1)}, bf16[512,1024]{1,0:T(8,128)(2,1)S(1)}, u32[]{:S(2)}, u32[]{:S(2)}) collective-permute-start(bf16[512,1024]{1,0:T(8,128)(2,1)S(1)} %get-tuple-element.96), channel_id=1, source_target_pairs={{0,1},{1,0},{2,3},{3,2},{4,5},{5,4},{6,7},{7,6},{8,9},{9,8},{10,11... | collective-permute-start | bytes 3145736 | tf_op jit(solution)/shard_map/ppermute | solution.py:17
  162.1 87.4 %reduce-scatter.8.cloned.1.call-start = ((), (), s32[]{:S(2)}) async-start(), calls=%async_computation.12 | async-start | bytes 1638400 | tf_op jit(solution)/shard_map/reduce_scatter | solution.py:384
  163.7 8.4 %collective-permute-start.26 = (bf16[128,1024]{1,0:T(8,128)(2,1)S(1)}, bf16[128,1024]{1,0:T(8,128)(2,1)S(1)}, u32[]{:S(2)}, u32[]{:S(2)}) collective-permute-start(bf16[128,1024]{1,0:T(8,128)(2,1)S(1)} %get-tuple-element.138), channel_id=1, source_target_pairs={{0,2},{1,3},{2,0},{3,1},{4,6},{5,7},{6,4},{7,5},{8,10},{9,11},{10,... | collective-permute-start | bytes 786440 | tf_op jit(solution)/shard_map/ppermute | solution.py:17
  165.2 9.2 %collective-permute-start.27 = (bf16[128,1024]{1,0:T(8,128)(2,1)S(1)}, bf16[128,1024]{1,0:T(8,128)(2,1)S(1)}, u32[]{:S(2)}, u32[]{:S(2)}) collective-permute-start(bf16[128,1024]{1,0:T(8,128)(2,1)S(1)} %get-tuple-element.140), channel_id=1, source_target_pairs={{0,4},{1,5},{2,6},{3,7},{4,0},{5,1},{6,2},{7,3},{8,12},{9,13},{10,... | collective-permute-start | bytes 786440 | tf_op jit(solution)/shard_map/ppermute | solution.py:17
  166.7 12.2 %collective-permute-start.28 = (bf16[128,1024]{1,0:T(8,128)(2,1)S(1)}, bf16[128,1024]{1,0:T(8,128)(2,1)S(1)}, u32[]{:S(2)}, u32[]{:S(2)}) collective-permute-start(bf16[128,1024]{1,0:T(8,128)(2,1)S(1)} %get-tuple-element.139), channel_id=1, source_target_pairs={{0,6},{1,7},{2,4},{3,5},{4,2},{5,3},{6,0},{7,1},{8,14},{9,15},{10,... | collective-permute-start | bytes 786440 | tf_op jit(solution)/shard_map/ppermute | solution.py:17
  181.3 8.5 %collective-permute-start.29 = (bf16[128,1024]{1,0:T(8,128)(2,1)}, bf16[128,1024]{1,0:T(8,128)(2,1)S(1)}, u32[]{:S(2)}, u32[]{:S(2)}) collective-permute-start(bf16[128,1024]{1,0:T(8,128)(2,1)} %get-tuple-element.118), channel_id=1, source_target_pairs={{0,2},{1,3},{2,0},{3,1},{4,6},{5,7},{6,4},{7,5},{8,10},{9,11},{10,... | collective-permute-start | bytes 786440 | tf_op jit(solution)/shard_map/ppermute | solution.py:17
  182.8 9.6 %collective-permute-start.30 = (bf16[128,1024]{1,0:T(8,128)(2,1)}, bf16[128,1024]{1,0:T(8,128)(2,1)}, u32[]{:S(2)}, u32[]{:S(2)}) collective-permute-start(bf16[128,1024]{1,0:T(8,128)(2,1)} %get-tuple-element.118), channel_id=1, source_target_pairs={{0,4},{1,5},{2,6},{3,7},{4,0},{5,1},{6,2},{7,3},{8,12},{9,13},{10,... | collective-permute-start | bytes 786440 | tf_op jit(solution)/shard_map/ppermute | solution.py:17
  184.2 11.4 %collective-permute-start.31 = (bf16[128,1024]{1,0:T(8,128)(2,1)}, bf16[128,1024]{1,0:T(8,128)(2,1)}, u32[]{:S(2)}, u32[]{:S(2)}) collective-permute-start(bf16[128,1024]{1,0:T(8,128)(2,1)} %get-tuple-element.118), channel_id=1, source_target_pairs={{0,6},{1,7},{2,4},{3,5},{4,2},{5,3},{6,0},{7,1},{8,14},{9,15},{10,... | collective-permute-start | bytes 786440 | tf_op jit(solution)/shard_map/ppermute | solution.py:17
  184.9 12.3 %collective-permute-start.32 = (bf16[128,1024]{1,0:T(8,128)(2,1)}, bf16[128,1024]{1,0:T(8,128)(2,1)}, u32[]{:S(2)}, u32[]{:S(2)}) collective-permute-start(bf16[128,1024]{1,0:T(8,128)(2,1)} %get-tuple-element.118), channel_id=1, source_target_pairs={{0,1},{1,0},{2,3},{3,2},{4,5},{5,4},{6,7},{7,6},{8,9},{9,8},{10,11... | collective-permute-start | bytes 786440 | tf_op jit(solution)/shard_map/ppermute | solution.py:17
  189.8 7.3 %collective-permute-start.33 = (bf16[128,1024]{1,0:T(8,128)(2,1)S(1)}, bf16[128,1024]{1,0:T(8,128)(2,1)}, u32[]{:S(2)}, u32[]{:S(2)}) collective-permute-start(bf16[128,1024]{1,0:T(8,128)(2,1)S(1)} %collective-permute-done.29), channel_id=1, source_target_pairs={{0,1},{1,0},{2,3},{3,2},{4,5},{5,4},{6,7},{7,6},{8,9},{9,8},{10,11... | collective-permute-start | bytes 786440 | tf_op jit(solution)/shard_map/ppermute | solution.py:17
  215.1 10.6 %collective-permute-start.40 = (bf16[512,1024]{1,0:T(8,128)(2,1)}, bf16[512,1024]{1,0:T(8,128)(2,1)}, u32[]{:S(2)}, u32[]{:S(2)}) collective-permute-start(bf16[512,1024]{1,0:T(8,128)(2,1)} %convolution_convert_fusion.1), channel_id=1, source_target_pairs={{0,1},{1,0},{2,3},{3,2},{4,5},{5,4},{6,7},{7,6},{8,9},{9,8},{10,11... | collective-permute-start | bytes 3145736 | tf_op jit(solution)/shard_map/ppermute | solution.py:17
  217.6 14.9 %collective-permute-start.36 = (bf16[512,1024]{1,0:T(8,128)(2,1)}, bf16[512,1024]{1,0:T(8,128)(2,1)}, u32[]{:S(2)}, u32[]{:S(2)}) collective-permute-start(bf16[512,1024]{1,0:T(8,128)(2,1)} %convolution_convert_fusion.2), channel_id=1, source_target_pairs={{0,1},{1,0},{2,3},{3,2},{4,5},{5,4},{6,7},{7,6},{8,9},{9,8},{10,11... | collective-permute-start | bytes 3145736 | tf_op jit(solution)/shard_map/ppermute | solution.py:17
  218.8 36.2 %all-to-all-start.3 = ((bf16[32,32,384]{2,1,0:T(8,128)(2,1)}), bf16[32,32,384]{2,1,0:T(8,128)(2,1)}, u32[]{:S(2)}, u32[]{:S(2)}) async-start(bf16[32,32,384]{2,1,0:T(8,128)(2,1)} %bitcast.276), calls=%async_computation.3 | async-start | bytes 1572864 | tf_op jit(solution)/shard_map/all_to_all | solution.py:419
  222.6 55.2 %reduce-scatter.4.cloned.1.call-start = ((), (), s32[]{:S(2)}) async-start(), calls=%async_computation.10 | async-start | bytes 1966080 | tf_op jit(solution)/shard_map/reduce_scatter | solution.py:430
  229.0 11.0 %collective-permute-start.41 = (bf16[128,1024]{1,0:T(8,128)(2,1)S(1)}, bf16[128,1024]{1,0:T(8,128)(2,1)S(1)}, u32[]{:S(2)}, u32[]{:S(2)}) collective-permute-start(bf16[128,1024]{1,0:T(8,128)(2,1)S(1)} %get-tuple-element.128), channel_id=1, source_target_pairs={{0,2},{1,3},{2,0},{3,1},{4,6},{5,7},{6,4},{7,5},{8,10},{9,11},{10,... | collective-permute-start | bytes 786440 | tf_op jit(solution)/shard_map/ppermute | solution.py:17
  230.7 11.5 %collective-permute-start.42 = (bf16[128,1024]{1,0:T(8,128)(2,1)S(1)}, bf16[128,1024]{1,0:T(8,128)(2,1)S(1)}, u32[]{:S(2)}, u32[]{:S(2)}) collective-permute-start(bf16[128,1024]{1,0:T(8,128)(2,1)S(1)} %get-tuple-element.130), channel_id=1, source_target_pairs={{0,4},{1,5},{2,6},{3,7},{4,0},{5,1},{6,2},{7,3},{8,12},{9,13},{10,... | collective-permute-start | bytes 786440 | tf_op jit(solution)/shard_map/ppermute | solution.py:17
  232.2 16.0 %collective-permute-start.43 = (bf16[128,1024]{1,0:T(8,128)(2,1)S(1)}, bf16[128,1024]{1,0:T(8,128)(2,1)S(1)}, u32[]{:S(2)}, u32[]{:S(2)}) collective-permute-start(bf16[128,1024]{1,0:T(8,128)(2,1)S(1)} %get-tuple-element.129), channel_id=1, source_target_pairs={{0,6},{1,7},{2,4},{3,5},{4,2},{5,3},{6,0},{7,1},{8,14},{9,15},{10,... | collective-permute-start | bytes 786440 | tf_op jit(solution)/shard_map/ppermute | solution.py:17
  235.1 25.0 %collective-permute-start.37 = (bf16[128,1024]{1,0:T(8,128)(2,1)S(1)}, bf16[128,1024]{1,0:T(8,128)(2,1)S(1)}, u32[]{:S(2)}, u32[]{:S(2)}) collective-permute-start(bf16[128,1024]{1,0:T(8,128)(2,1)S(1)} %get-tuple-element.135), channel_id=1, source_target_pairs={{0,2},{1,3},{2,0},{3,1},{4,6},{5,7},{6,4},{7,5},{8,10},{9,11},{10,... | collective-permute-start | bytes 786440 | tf_op jit(solution)/shard_map/ppermute | solution.py:17
  236.8 23.3 %collective-permute-start.38 = (bf16[128,1024]{1,0:T(8,128)(2,1)S(1)}, bf16[128,1024]{1,0:T(8,128)(2,1)S(1)}, u32[]{:S(2)}, u32[]{:S(2)}) collective-permute-start(bf16[128,1024]{1,0:T(8,128)(2,1)S(1)} %get-tuple-element.137), channel_id=1, source_target_pairs={{0,4},{1,5},{2,6},{3,7},{4,0},{5,1},{6,2},{7,3},{8,12},{9,13},{10,... | collective-permute-start | bytes 786440 | tf_op jit(solution)/shard_map/ppermute | solution.py:17
  240.0 20.1 %collective-permute-start.39 = (bf16[128,1024]{1,0:T(8,128)(2,1)S(1)}, bf16[128,1024]{1,0:T(8,128)(2,1)S(1)}, u32[]{:S(2)}, u32[]{:S(2)}) collective-permute-start(bf16[128,1024]{1,0:T(8,128)(2,1)S(1)} %get-tuple-element.136), channel_id=1, source_target_pairs={{0,6},{1,7},{2,4},{3,5},{4,2},{5,3},{6,0},{7,1},{8,14},{9,15},{10,... | collective-permute-start | bytes 786440 | tf_op jit(solution)/shard_map/ppermute | solution.py:17
  255.0 15.4 %all-to-all-start.4 = ((bf16[8,2,32,576]{3,2,1,0:T(8,128)(2,1)}), bf16[8,2,32,576]{3,2,1,0:T(8,128)(2,1)}, u32[]{:S(2)}, u32[]{:S(2)}) async-start(bf16[8,2,32,576]{3,2,1,0:T(8,128)(2,1)} %maximum_bitcast_fusion), calls=%async_computation.7 | async-start | bytes 1310720 | tf_op jit(solution)/shard_map/all_to_all | solution.py:429
  (88 other events, 382.1 us)
Sparse Core Ops, SparseCore 0:
  19.6 49.8 all-gather.8
  71.6 33.2 all-gather.4
  107.1 31.6 all-gather.6
  162.3 30.1 reduce-scatter.5
  196.0 30.3 reduce-scatter.7
  228.6 38.3 reduce-scatter.3
